TPU v7x, 256 devices: a whole 4x4x8 slice. The times are simulated.
256 devices in a mesh: tmpl: 32 (over y, x, core), sta: 8 (over z).
Axes of the slice: x: 4, y: 4, z: 8, core: 2. Of those that a mesh axis runs over, the one named last changes fastest.
Arguments:
- records: bfloat16 [64, 1024, 3, 512], P('sta', 'tmpl'), may hold values from -40 to 40
- templates: bfloat16 [16384, 3, 512], P('tmpl'), may hold values from -40 to 40
- requests: int32 [32, 32, 4], P('tmpl'), may hold values from 0 to 31, as said below
- pair_slot: int32 [16384], P('tmpl'), may hold values from 0 to 127
- pair_template: int32 [16384], P('tmpl'), may hold values from 0 to 31, as said below
- pair_offset: int32 [16384], P('tmpl'), may hold values from 0 to 511
- live_pairs: int32 [32], P('tmpl'), may hold values from 32 to 512, as said below
Outputs:
- stacks: float32 [64, 1024, 512], P('sta', 'tmpl')
Inputs may be any that keep to these rules, and one draw needn't show every extreme that they name: `requests`: for each owner and index of tmpl, 4 different local station numbers. `pair_template`: each owner's first 32 pair slots name its 32 templates once each. `live_pairs`: the busiest owner holds 512 live pairs.
All inputs are finite; a program needn't handle non-finite values.
Results may differ from a plain program's by a relative error of at most 0.013.
Values may be sent and summed in bfloat16 or wider, within the bound.
A program may use at most 128 MiB of HBM per device.

v0:
```python
import math

import jax
import jax.numpy as jnp
from jax import lax
from jax.sharding import PartitionSpec as P

T_DEV = 32


epsilon = 1e-05


def from_behind(value, axis, steps):
    count = lax.axis_size(axis)
    leading, last = (max(0, -steps), min(count, count - steps))
    return lax.ppermute(value, axis, [(source, source + steps) for source in range(leading, last)])


def dft_tables(length):
    full_length = 2 * length
    sample_ids = jnp.arange(full_length, dtype=jnp.int32)[:, None]
    frequency = jnp.arange(length, dtype=jnp.int32)[None, :]
    phases = (sample_ids * frequency % full_length).astype(jnp.float32) * (
        2.0 * jnp.pi / full_length
    )
    parity = jnp.where(sample_ids % 2 == 0, 1.0, -1.0).astype(jnp.float32)
    second = jnp.where(frequency == 0, parity, -jnp.sin(phases))
    forward = jnp.concatenate([jnp.cos(phases), second], axis=1).astype(jnp.bfloat16)
    bin_ids = jnp.arange(length, dtype=jnp.int32)[:, None]
    lag_ids = jnp.arange(length, dtype=jnp.int32)[None, :]
    angles = (bin_ids * lag_ids % full_length).astype(jnp.float32) * (2.0 * jnp.pi / full_length)
    alternate = jnp.where(lag_ids % 2 == 0, 1.0, -1.0).astype(jnp.float32)
    cosine_rows = jnp.where(bin_ids == 0, 1.0, 2.0 * jnp.cos(angles)) / full_length
    sine_rows = jnp.where(bin_ids == 0, alternate, -2.0 * jnp.sin(angles)) / full_length
    inverse = jnp.concatenate([cosine_rows, sine_rows], axis=0).astype(jnp.bfloat16)
    return (forward, inverse)


def cross_spectrum(template_spec, station_spec):
    length = template_spec.shape[-1] // 2
    left = template_spec.astype(jnp.float32)
    right = station_spec.astype(jnp.float32)
    left_real, left_imag = (left[..., :length], left[..., length:])
    right_real, right_imag = (right[..., :length], right[..., length:])
    zero_bin = jnp.arange(length) == 0
    paired = left_imag * right_imag
    real_part = left_real * right_real + jnp.where(zero_bin, 0.0, paired)
    imag_part = jnp.where(zero_bin, paired, left_real * right_imag - left_imag * right_real)
    return jnp.sum(jnp.concatenate([real_part, imag_part], axis=-1), axis=-2)


def station_spectra(hop_rows, forward):
    length = hop_rows.shape[-1]
    windows = jnp.concatenate([hop_rows[:, :-1], hop_rows[:, 1:]], axis=-1)
    spectra = jnp.dot(windows.reshape(-1, 2 * length), forward, preferred_element_type=jnp.float32)
    spectra = spectra.astype(jnp.bfloat16).reshape(windows.shape)
    squares = jnp.sum(jnp.square(hop_rows.astype(jnp.float32)), axis=2)
    sample_ids = jnp.arange(length, dtype=jnp.int32)[:, None]
    lag_ids = jnp.arange(length, dtype=jnp.int32)[None, :]
    later = (sample_ids >= lag_ids).astype(jnp.float32)
    earlier = (sample_ids < lag_ids).astype(jnp.float32)
    energy = jnp.dot(squares[:, :-1], later, precision=lax.Precision.HIGHEST)
    energy = energy + jnp.dot(squares[:, 1:], earlier, precision=lax.Precision.HIGHEST)
    return (spectra, energy)


def shift_rows(flattened, shifts, length, kept_samples):
    row_count = flattened.shape[0]
    sections = max(1, (length - 1).bit_length())
    for section in range(sections):
        step = 1 << section
        moved = jnp.concatenate(
            [flattened[:, step:], jnp.zeros((row_count, step), flattened.dtype)], axis=1
        )
        chosen = jnp.right_shift(shifts, section) & 1 == 1
        flattened = jnp.where(chosen[:, None], moved, flattened)
    return flattened[:, :kept_samples]


def shards(records, templates, requests, pair_slot, pair_template, pair_offset, live_pairs):
    hops_here, stations_here, components, length = records.shape
    pairs_here = templates.shape[0]
    forward, inverse = dft_tables(length)
    ahead = from_behind(records[:2], "sta", -1)
    hop_rows = jnp.transpose(jnp.concatenate([records, ahead], axis=0), (1, 0, 2, 3))
    own_spectra, own_energy = station_spectra(hop_rows, forward)
    wanted = lax.all_to_all(requests[0], "tmpl", split_axis=0, concat_axis=0, tiled=True)
    spectra_part = lax.all_to_all(
        own_spectra[wanted], "tmpl", split_axis=0, concat_axis=0, tiled=True
    )
    energy_part = lax.all_to_all(
        own_energy[wanted], "tmpl", split_axis=0, concat_axis=0, tiled=True
    )
    fetched = (spectra_part, energy_part)
    got_spectra = fetched[0].reshape((-1,) + fetched[0].shape[2:])
    got_energy = fetched[1].reshape((-1,) + fetched[1].shape[2:])
    block_rows = math.gcd(pairs_here, 64)
    live_count = live_pairs[0]
    turns = (live_count + block_rows - 1) // block_rows
    length_scale = 3.0 * length
    template_ids = jnp.arange(T_DEV, dtype=jnp.int32)
    kept_samples = hops_here * length
    forward_short = forward[:length]

    def accumulate(turn_index, running):
        first_row = turn_index * block_rows
        shapes = lax.dynamic_slice_in_dim(templates, first_row, block_rows, 0)
        slot_ids = lax.dynamic_slice_in_dim(pair_slot, first_row, block_rows, 0)
        owners_ids = lax.dynamic_slice_in_dim(pair_template, first_row, block_rows, 0)
        shifts = lax.dynamic_slice_in_dim(pair_offset, first_row, block_rows, 0)
        template_spec = jnp.dot(
            shapes.reshape(-1, length), forward_short, preferred_element_type=jnp.float32
        )
        template_spec = template_spec.astype(jnp.bfloat16).reshape(
            block_rows, components, 2 * length
        )
        template_energy = jnp.sum(jnp.square(shapes.astype(jnp.float32)), axis=(1, 2))
        product = cross_spectrum(template_spec[:, None], got_spectra[slot_ids]).astype(jnp.bfloat16)
        lagged = jnp.dot(product, inverse, preferred_element_type=jnp.float32)
        denominator = length_scale * jnp.sqrt(
            (got_energy[slot_ids] / length_scale + epsilon)
            * (template_energy[:, None, None] / length_scale + epsilon)
        )
        flattened = (lagged / denominator).reshape(block_rows, -1)
        shifted = shift_rows(flattened, shifts, length, kept_samples)
        row_ids = first_row + jnp.arange(block_rows, dtype=jnp.int32)
        weights = (
            (owners_ids[:, None] == template_ids[None, :]) & (row_ids < live_count)[:, None]
        ).astype(jnp.float32)
        return running + jnp.dot(weights.T, shifted, precision=lax.Precision.HIGHEST)

    running = lax.fori_loop(0, turns, accumulate, jnp.zeros((T_DEV, kept_samples), jnp.float32))
    live_rows = jnp.arange(pairs_here, dtype=jnp.int32) < live_count
    counts = jnp.sum(
        ((pair_template[:, None] == template_ids[None, :]) & live_rows[:, None]).astype(
            jnp.float32
        ),
        axis=0,
    )
    stacked = running * jnp.sqrt(length_scale / counts)[:, None]
    return jnp.transpose(stacked.reshape(T_DEV, hops_here, length), (1, 0, 2))


def solution(mesh):
    in_specs = (
        P("sta", "tmpl", None, None),
        P("tmpl", None, None),
        P("tmpl", None, None),
        P("tmpl"),
        P("tmpl"),
        P("tmpl"),
        P("tmpl"),
    )
    out_specs = P("sta", "tmpl", None)
    return jax.shard_map(shards, mesh=mesh, in_specs=in_specs, out_specs=out_specs, check_vma=False)
```

profile of v0, /device:TPU:104, one launch (start us, length us, event | category | flops | bytes accessed | tf_op | source)
XLA Modules:
  0.0 588.0 jit_solution(3651733538250807918)
XLA Ops:
  1.4 7.5 %all-to-all-start = ((s32[32,1,4]{2,1,0:T(1,128)}), s32[32,1,4]{2,1,0:T(1,128)S(1)}, u32[]{:S(2)}, u32[]{:S(2)}) async-start(s32[32,1,4]{2,1,0:T(1,128)} %copy.65), calls=%async_computation | async-start | bytes 32768 | tf_op jit(solution)/shard_map/all_to_all | solution.py:88
  26.0 5.6 copy.71
  31.6 8.1 %all-to-all-start.2 = ((f32[32,4,9,512]{3,1,2,0:T(4,128)}), f32[32,4,9,512]{3,1,2,0:T(4,128)}, u32[]{:S(2)}, u32[]{:S(2)}) async-start(f32[32,4,9,512]{3,1,2,0:T(4,128)} %copy.71), calls=%async_computation.2 | async-start | bytes 4718592 | tf_op jit(solution)/shard_map/all_to_all | solution.py:92
  39.8 7.9 %cosine_convert_fusion = bf16[1024,512]{1,0:T(8,128)(2,1)S(1)} fusion(), kind=kLoop, calls=%fused_computation.66 | loop fusion | flops 7864320 | bytes 1048576 | tf_op jit(solution)/shard_map/convert.3
  47.6 8.8 %select_convert_fusion = bf16[1024,512]{1,0:T(8,128)(2,1)} fusion(bf16[1024]{0:T(1024)(128)(2,1)S(1)} %fusion.45, pred[512]{0:T(512)(128)(4,1)S(1)} %iota_compare_fusion.6), kind=kLoop, calls=%fused_computation.65 | loop fusion | flops 8388608 | bytes 1051136 | tf_op jit(solution)/shard_map/convert.4
  70.4 11.9 %gather_fusion.2 = bf16[128,9,3,1024]{3,2,1,0:T(4,128)(2,1)} fusion(bf16[32,9,3,1024]{3,2,1,0:T(4,128)(2,1)S(1)} %reshape.147, s32[1024]{0:T(1024)S(1)} %pad_clamp_fusion.1), kind=kCustom, calls=%fused_computation.2 | custom fusion | bytes 14156288 | tf_op jit(solution)/shard_map/gather | solution.py:90
  82.3 13.8 %copy.68 = bf16[32,4,9,3,1024]{4,1,3,2,0:T(4,128)(2,1)} copy(bf16[32,4,9,3,1024]{4,3,2,1,0:T(4,128)(2,1)} %bitcast.57) | data formatting | bytes 14155776 | tf_op jit(solution)/shard_map/gather | solution.py:90
  96.1 7.6 %all-to-all-start.1 = ((bf16[32,4,9,3,1024]{4,1,3,2,0:T(4,128)(2,1)}), bf16[32,4,9,3,1024]{4,1,3,2,0:T(4,128)(2,1)}, u32[]{:S(2)}, u32[]{:S(2)}) async-start(bf16[32,4,9,3,1024]{4,1,3,2,0:T(4,128)(2,1)} %copy.68), calls=%async_computation.1 | async-start | bytes 14155776 | tf_op jit(solution)/shard_map/all_to_all | solution.py:89
  115.7 73.0 %all-to-all-done.1 = bf16[32,4,9,3,1024]{4,1,3,2,0:T(4,128)(2,1)} async-done(((bf16[32,4,9,3,1024]{4,1,3,2,0:T(4,128)(2,1)}), bf16[32,4,9,3,1024]{4,1,3,2,0:T(4,128)(2,1)}, u32[]{:S(2)}, u32[]{:S(2)}) %all-to-all-start.1) | async-done | bytes 7077920 | tf_op jit(solution)/shard_map/all_to_all | solution.py:89
  188.7 10.3 %copy.77 = bf16[32,4,9,3,1024]{4,3,2,1,0:T(4,128)(2,1)} copy(bf16[32,4,9,3,1024]{4,1,3,2,0:T(4,128)(2,1)} %all-to-all-done.1) | data formatting | bytes 14155776
  199.8 385.4 %while.11 = (s32[]{:T(128)}, f32[32,4096]{1,0:T(8,128)}, s32[]{:T(128)}, s32[512]{0:T(512)S(1)}, s32[]{:T(128)}, /*index=5*/s32[512]{0:T(512)}, bf16[512,3,512]{...) while((s32[]{:T(128)}, f32[32,4096]{1,0:T(8,128)}, ...), condition=%wide.region_4.5_spmd.clone, body=%wide.region_1.4_spmd.clone.sunk | while | flops 922689088 | bytes 121778384 | solution.py:133
  204.2 10.6 %gather_fusion = bf16[64,9,3,1024]{3,2,1,0:T(4,128)(2,1)} fusion(bf16[128,9,3,1024]{3,2,1,0:T(4,128)(2,1)} %get-tuple-element.349, s32[1024]{0:T(1024)S(1)} %pad_clamp_fusion.3), kind=kCustom, calls=%fused_computation.clone.clone.1 | custom fusion | bytes 7078144 | tf_op jit(solution)/shard_map/while/body/gather | solution.py:119
  214.9 5.1 convert_element_type.92
  224.5 8.4 %maximum_reduce_fusion.2 = bf16[64,9,1024]{2,1,0:T(8,128)(2,1)} fusion(f32[64,9,3,512]{3,2,1,0:T(4,128)S(1)} %get-tuple-element.295, f32[64,9,3,512]{3,2,1,0:T(4,128)S(1)} %get-tuple-element.296), kind=kLoop, calls=%fused_computation.5.clone.1 | loop fusion | flops 2949120 | bytes 8257536 | tf_op jit(solution)/shard_map/while/body/reduce_sum | solution.py:50
  252.3 10.6 %gather_fusion = bf16[64,9,3,1024]{3,2,1,0:T(4,128)(2,1)} fusion(bf16[128,9,3,1024]{3,2,1,0:T(4,128)(2,1)} %get-tuple-element.349, s32[1024]{0:T(1024)S(1)} %pad_clamp_fusion.3), kind=kCustom, calls=%fused_computation.clone.clone.1 | custom fusion | bytes 7078144 | tf_op jit(solution)/shard_map/while/body/gather | solution.py:119
  263.0 5.1 convert_element_type.92
  272.6 8.4 %maximum_reduce_fusion.2 = bf16[64,9,1024]{2,1,0:T(8,128)(2,1)} fusion(f32[64,9,3,512]{3,2,1,0:T(4,128)S(1)} %get-tuple-element.295, f32[64,9,3,512]{3,2,1,0:T(4,128)S(1)} %get-tuple-element.296), kind=kLoop, calls=%fused_computation.5.clone.1 | loop fusion | flops 2949120 | bytes 8257536 | tf_op jit(solution)/shard_map/while/body/reduce_sum | solution.py:50
  300.4 10.6 %gather_fusion = bf16[64,9,3,1024]{3,2,1,0:T(4,128)(2,1)} fusion(bf16[128,9,3,1024]{3,2,1,0:T(4,128)(2,1)} %get-tuple-element.349, s32[1024]{0:T(1024)S(1)} %pad_clamp_fusion.3), kind=kCustom, calls=%fused_computation.clone.clone.1 | custom fusion | bytes 7078144 | tf_op jit(solution)/shard_map/while/body/gather | solution.py:119
  311.1 5.1 convert_element_type.92
  320.7 8.4 %maximum_reduce_fusion.2 = bf16[64,9,1024]{2,1,0:T(8,128)(2,1)} fusion(f32[64,9,3,512]{3,2,1,0:T(4,128)S(1)} %get-tuple-element.295, f32[64,9,3,512]{3,2,1,0:T(4,128)S(1)} %get-tuple-element.296), kind=kLoop, calls=%fused_computation.5.clone.1 | loop fusion | flops 2949120 | bytes 8257536 | tf_op jit(solution)/shard_map/while/body/reduce_sum | solution.py:50
  348.5 10.6 %gather_fusion = bf16[64,9,3,1024]{3,2,1,0:T(4,128)(2,1)} fusion(bf16[128,9,3,1024]{3,2,1,0:T(4,128)(2,1)} %get-tuple-element.349, s32[1024]{0:T(1024)S(1)} %pad_clamp_fusion.3), kind=kCustom, calls=%fused_computation.clone.clone.1 | custom fusion | bytes 7078144 | tf_op jit(solution)/shard_map/while/body/gather | solution.py:119
  359.2 5.1 convert_element_type.92
  368.8 8.4 %maximum_reduce_fusion.2 = bf16[64,9,1024]{2,1,0:T(8,128)(2,1)} fusion(f32[64,9,3,512]{3,2,1,0:T(4,128)S(1)} %get-tuple-element.295, f32[64,9,3,512]{3,2,1,0:T(4,128)S(1)} %get-tuple-element.296), kind=kLoop, calls=%fused_computation.5.clone.1 | loop fusion | flops 2949120 | bytes 8257536 | tf_op jit(solution)/shard_map/while/body/reduce_sum | solution.py:50
  396.7 10.6 %gather_fusion = bf16[64,9,3,1024]{3,2,1,0:T(4,128)(2,1)} fusion(bf16[128,9,3,1024]{3,2,1,0:T(4,128)(2,1)} %get-tuple-element.349, s32[1024]{0:T(1024)S(1)} %pad_clamp_fusion.3), kind=kCustom, calls=%fused_computation.clone.clone.1 | custom fusion | bytes 7078144 | tf_op jit(solution)/shard_map/while/body/gather | solution.py:119
  407.3 5.1 convert_element_type.92
  417.0 8.4 %maximum_reduce_fusion.2 = bf16[64,9,1024]{2,1,0:T(8,128)(2,1)} fusion(f32[64,9,3,512]{3,2,1,0:T(4,128)S(1)} %get-tuple-element.295, f32[64,9,3,512]{3,2,1,0:T(4,128)S(1)} %get-tuple-element.296), kind=kLoop, calls=%fused_computation.5.clone.1 | loop fusion | flops 2949120 | bytes 8257536 | tf_op jit(solution)/shard_map/while/body/reduce_sum | solution.py:50
  444.8 10.6 %gather_fusion = bf16[64,9,3,1024]{3,2,1,0:T(4,128)(2,1)} fusion(bf16[128,9,3,1024]{3,2,1,0:T(4,128)(2,1)} %get-tuple-element.349, s32[1024]{0:T(1024)S(1)} %pad_clamp_fusion.3), kind=kCustom, calls=%fused_computation.clone.clone.1 | custom fusion | bytes 7078144 | tf_op jit(solution)/shard_map/while/body/gather | solution.py:119
  465.1 8.4 %maximum_reduce_fusion.2 = bf16[64,9,1024]{2,1,0:T(8,128)(2,1)} fusion(f32[64,9,3,512]{3,2,1,0:T(4,128)S(1)} %get-tuple-element.295, f32[64,9,3,512]{3,2,1,0:T(4,128)S(1)} %get-tuple-element.296), kind=kLoop, calls=%fused_computation.5.clone.1 | loop fusion | flops 2949120 | bytes 8257536 | tf_op jit(solution)/shard_map/while/body/reduce_sum | solution.py:50
  492.9 10.6 %gather_fusion = bf16[64,9,3,1024]{3,2,1,0:T(4,128)(2,1)} fusion(bf16[128,9,3,1024]{3,2,1,0:T(4,128)(2,1)} %get-tuple-element.349, s32[1024]{0:T(1024)S(1)} %pad_clamp_fusion.3), kind=kCustom, calls=%fused_computation.clone.clone.1 | custom fusion | bytes 7078144 | tf_op jit(solution)/shard_map/while/body/gather | solution.py:119
  513.2 8.4 %maximum_reduce_fusion.2 = bf16[64,9,1024]{2,1,0:T(8,128)(2,1)} fusion(f32[64,9,3,512]{3,2,1,0:T(4,128)S(1)} %get-tuple-element.295, f32[64,9,3,512]{3,2,1,0:T(4,128)S(1)} %get-tuple-element.296), kind=kLoop, calls=%fused_computation.5.clone.1 | loop fusion | flops 2949120 | bytes 8257536 | tf_op jit(solution)/shard_map/while/body/reduce_sum | solution.py:50
  541.0 10.6 %gather_fusion = bf16[64,9,3,1024]{3,2,1,0:T(4,128)(2,1)} fusion(bf16[128,9,3,1024]{3,2,1,0:T(4,128)(2,1)} %get-tuple-element.349, s32[1024]{0:T(1024)S(1)} %pad_clamp_fusion.3), kind=kCustom, calls=%fused_computation.clone.clone.1 | custom fusion | bytes 7078144 | tf_op jit(solution)/shard_map/while/body/gather | solution.py:119
  561.3 8.4 %maximum_reduce_fusion.2 = bf16[64,9,1024]{2,1,0:T(8,128)(2,1)} fusion(f32[64,9,3,512]{3,2,1,0:T(4,128)S(1)} %get-tuple-element.295, f32[64,9,3,512]{3,2,1,0:T(4,128)S(1)} %get-tuple-element.296), kind=kLoop, calls=%fused_computation.5.clone.1 | loop fusion | flops 2949120 | bytes 8257536 | tf_op jit(solution)/shard_map/while/body/reduce_sum | solution.py:50
  (400 shorter events, 252.7 us)
Async XLA Ops:
  1.4 13.6 %all-to-all-start = ((s32[32,1,4]{2,1,0:T(1,128)}), s32[32,1,4]{2,1,0:T(1,128)S(1)}, u32[]{:S(2)}, u32[]{:S(2)}) async-start(s32[32,1,4]{2,1,0:T(1,128)} %copy.65), calls=%async_computation | async-start | bytes 32768 | tf_op jit(solution)/shard_map/all_to_all | solution.py:88
  9.9 10.2 %collective-permute-start = (bf16[2,32,3,512]{3,1,2,0:T(8,128)(2,1)S(1)}, bf16[2,32,3,512]{3,1,2,0:T(8,128)(2,1)S(1)}, u32[]{:S(2)}, u32[]{:S(2)}) collective-permute-start(bf16[2,32,3,512]{3,1,2,0:T(8,128)(2,1)S(1)} %slice.61), channel_id=1, source_target_pairs={{1,0},{2,1},{3,2},{4,3},{5,4},{6,5},{7,6},{9,8},{10,9},{11,10},{12... | collective-permute-start | bytes 589832 | tf_op jit(solution)/shard_map/ppermute | solution.py:17
  31.6 64.5 %all-to-all-start.2 = ((f32[32,4,9,512]{3,1,2,0:T(4,128)}), f32[32,4,9,512]{3,1,2,0:T(4,128)}, u32[]{:S(2)}, u32[]{:S(2)}) async-start(f32[32,4,9,512]{3,1,2,0:T(4,128)} %copy.71), calls=%async_computation.2 | async-start | bytes 4718592 | tf_op jit(solution)/shard_map/all_to_all | solution.py:92
  39.7 16.7 %copy-start.5 = (bf16[8,32,3,512]{3,1,2,0:T(8,128)(2,1)S(1)}, bf16[8,32,3,512]{3,1,2,0:T(8,128)(2,1)}, u32[]{:S(2)}) copy-start(bf16[8,32,3,512]{3,1,2,0:T(8,128)(2,1)} %param.9) | copy-start | bytes 2359300
  96.1 8.3 %copy-start.6 = (s32[512]{0:T(512)S(1)}, s32[512]{0:T(512)}, u32[]{:S(2)}) copy-start(s32[512]{0:T(512)} %param.13) | copy-start | bytes 6148
  96.1 8.4 %copy-start.4 = (bf16[1024,512]{1,0:T(8,128)(2,1)S(1)}, bf16[1024,512]{1,0:T(8,128)(2,1)}, u32[]{:S(2)}) copy-start(bf16[1024,512]{1,0:T(8,128)(2,1)} %select_convert_fusion) | copy-start | bytes 3145732
  96.1 92.6 %all-to-all-start.1 = ((bf16[32,4,9,3,1024]{4,1,3,2,0:T(4,128)(2,1)}), bf16[32,4,9,3,1024]{4,1,3,2,0:T(4,128)(2,1)}, u32[]{:S(2)}, u32[]{:S(2)}) async-start(bf16[32,4,9,3,1024]{4,1,3,2,0:T(4,128)(2,1)} %copy.68), calls=%async_computation.1 | async-start | bytes 14155776 | tf_op jit(solution)/shard_map/all_to_all | solution.py:89
  199.8 385.4 %copy-start.7 = (f32[32]{0:T(128)S(1)}, f32[32]{0:T(128)}, u32[]{:S(2)}) copy-start(f32[32]{0:T(128)} %divide_sqrt_fusion) | copy-start | bytes 388
  200.0 1.6 copy-start
  245.5 1.0 copy-start.2
  245.8 2.4 copy-start.1
  248.2 1.5 copy-start
  293.6 1.0 copy-start.2
  293.9 2.4 copy-start.1
  296.3 1.5 copy-start
  341.7 1.0 copy-start.2
  342.0 2.4 copy-start.1
  344.4 1.5 copy-start
  389.9 1.0 copy-start.2
  390.1 2.4 copy-start.1
  392.5 1.5 copy-start
  438.0 1.0 copy-start.2
  438.2 2.4 copy-start.1
  440.6 1.5 copy-start
  486.1 1.0 copy-start.2
  486.3 2.4 copy-start.1
  488.7 1.5 copy-start
  534.2 1.0 copy-start.2
  534.5 2.4 copy-start.1
  536.8 1.5 copy-start
  582.3 1.0 copy-start.2
  582.6 2.4 copy-start.1
  (8 other events, 6.4 us)
where the time goes:
time: 595 us; the launch traced here: 588 us
  local copies, waits for them, and re-layouts  230 us (39%)
  other arithmetic  204 us (34%)
  waiting for transfers between devices  80.9 us (14%)
  matrix products  44.6 us (7%)
  starting transfers between devices  25.3 us (4%)
    gather x8, local copies, waits for them, and re-layouts, accumulate(): got_spectra[slot_ids]  85 us
    all_to_all x1, waiting for transfers between devices, shards(): lax.all_to_all(own_spectra[wanted], 'tmpl', split_axis=0, concat_axis=0,...  73 us
    reduce_sum x8, other arithmetic, cross_spectrum(): return jnp.sum(jnp.concatenate([real_part, imag_part], axis=-1), axis=-2)  67 us
    convert_element_type x8, other arithmetic, cross_spectrum(): right = station_spec.astype(jnp.float32)  40.9 us
    add x8, other arithmetic, cross_spectrum(): real_part = left_real * right_real + jnp.where(zero_bin, 0.0, paired)  36.2 us
    dot_general x8, matrix products, accumulate(): lagged = jnp.dot(product, inverse, preferred_element_type=jnp.float32)  28.9 us
    gather x2, local copies, waits for them, and re-layouts, shards(): own_spectra[wanted]  25.7 us
    gather x8, local copies, waits for them, and re-layouts, accumulate(): got_energy[slot_ids] / length_scale + epsilon  22.9 us
  transfers between devices with their start and end apart: 4, of which 3 were waited for; matrix products, arithmetic and copies ran while one was open for 12% of the time, Pallas kernels for 0%

commit v1 on v0

v1 whole, which is shorter than its diff:
```python
import functools

import jax
import jax.numpy as jnp
import numpy as np
from jax import lax
from jax.experimental import pallas as pl
from jax.experimental.pallas import tpu as pltpu
from jax.sharding import PartitionSpec as P

TL = 512
NBINS = 2 * TL
T_DEV = 32
FETCH = 4
SCALE = 3.0 * TL
EPSILON = 1e-05
MESH = pl.DeviceIdType.MESH
PB = 16


def dft_tables():
    n = np.arange(TL)[:, None]
    k = np.arange(TL)[None, :]
    angles = (n * k % NBINS) * (2.0 * np.pi / NBINS)
    parity = np.where(n % 2 == 0, 1.0, -1.0)
    second = np.where(k == 0, parity, -np.sin(angles))
    forward = np.concatenate([np.cos(angles), second], axis=1).astype(jnp.bfloat16)
    alternate = np.where(k % 2 == 0, 1.0, -1.0)
    cosine_rows = np.where(n == 0, 1.0, 2.0 * np.cos(angles)) / NBINS
    sine_rows = np.where(n == 0, alternate, -2.0 * np.sin(angles)) / NBINS
    inverse = np.concatenate([cosine_rows, sine_rows], axis=0).astype(jnp.bfloat16)
    return forward, inverse


FORWARD, INVERSE = dft_tables()

GROUPS = 8
PER = 4
ROWS = FETCH * 24


def split(value):
    high = value.astype(jnp.bfloat16)
    low = (value - high.astype(jnp.float32)).astype(jnp.bfloat16)
    return high, low


def mm(left, right):
    return jnp.dot(left, right, preferred_element_type=jnp.float32)


def exchange_kernel(
    count, depth, rec_ref, ask_ref, tmp_ref, fwd_ref, spec_out, rs_out, t_out,
    rec32, asked, wanted, send, recv, halo_send, halo_recv, parts, part_energy, halo_spec,
    spec, rs, temps,
    ask_send_sem, ask_recv_sem, send_sem, recv_sem, halo_send_sem, halo_recv_sem, local_sem,
):
    me = lax.axis_index("tmpl")
    z = lax.axis_index("sta")
    above = lax.rem(z + 1, depth)
    below = lax.rem(z + depth - 1, depth)

    def ahead(i):
        return lax.rem(me + i, count)

    def behind(i):
        return lax.rem(me + count - i, count)

    barrier = pltpu.get_barrier_semaphore()

    def greet(i, carry):
        pl.semaphore_signal(barrier, inc=1, device_id={"tmpl": ahead(i)}, device_id_type=MESH)
        return carry

    lax.fori_loop(1, count, greet, 0)
    pl.semaphore_signal(barrier, inc=1, device_id={"sta": above}, device_id_type=MESH)
    pl.semaphore_signal(barrier, inc=1, device_id={"sta": below}, device_id_type=MESH)

    def widen(i, carry):
        block = rec_ref[i].astype(jnp.float32)
        for g in range(4):
            rec32[g, pl.ds(pl.multiple_of(i * 32, 32), 32), :] = block[:, g * 128:(g + 1) * 128]
        return carry

    lax.fori_loop(0, 24, widen, 0)
    pl.semaphore_wait(barrier, count + 1)

    def ask_copy(i):
        return pltpu.make_async_remote_copy(
            src_ref=ask_ref.at[ahead(i)], dst_ref=asked.at[i],
            send_sem=ask_send_sem.at[i], recv_sem=ask_recv_sem.at[i],
            device_id={"tmpl": ahead(i)}, device_id_type=MESH,
        )

    def ask_start(i, carry):
        ask_copy(i).start()
        return carry

    lax.fori_loop(1, count, ask_start, 0)
    asked[0] = ask_ref[me]

    lane = lax.broadcasted_iota(jnp.int32, (128, 128), 1)

    def template_block(n, carry):
        first = pl.multiple_of(n * 128, 128)
        pieces = [tmp_ref[c, pl.ds(first, 128), :] for c in range(3)]
        energy = sum(jnp.sum(jnp.square(p.astype(jnp.float32)), axis=1, keepdims=True) for p in pieces)
        factor = lax.rsqrt(energy / SCALE + EPSILON) / SCALE
        for c in range(3):
            found = mm(pieces[c], fwd_ref[...]) * factor
            for g in range(4):
                base = n * 4096 + g * 8
                temps[pl.ds(base + c, 128, stride=32), :] = found[:, g * 128:(g + 1) * 128]
                temps[pl.ds(base + c + 3, 128, stride=32), :] = found[:, TL + g * 128:TL + (g + 1) * 128]
        for g in range(4):
            for row in (6, 7):
                temps[pl.ds(n * 4096 + g * 8 + row, 128, stride=32), :] = jnp.zeros((128, 128), jnp.float32)
        return carry

    def ask_wait(i, carry):
        ask_copy(i).wait()
        return carry

    lax.fori_loop(1, count, ask_wait, 0)
    to_scalar = pltpu.make_async_copy(asked, wanted, local_sem.at[0])
    to_scalar.start()
    to_scalar.wait()

    def gather(i):
        rows = []
        for f in range(FETCH):
            s = wanted[i, 0, f]
            for c in range(3):
                rows.append(
                    jnp.concatenate(
                        [rec32[g, pl.ds(c * 32 + s, 8, stride=96), :] for g in range(4)], axis=1
                    )
                )
        return jnp.concatenate(rows, axis=0).astype(jnp.bfloat16)

    def data_copy(i):
        return pltpu.make_async_remote_copy(
            src_ref=send.at[i], dst_ref=recv.at[i],
            send_sem=send_sem.at[i], recv_sem=recv_sem.at[i],
            device_id={"tmpl": behind(i)}, device_id_type=MESH,
        )

    def data_start(i, carry):
        send[i] = gather(i)
        data_copy(i).start()
        return carry

    lax.fori_loop(1, count, data_start, 0)
    recv[0] = gather(0)

    lax.fori_loop(0, 4, template_block, 0)
    out_t = pltpu.make_async_copy(temps, t_out, local_sem.at[1])
    out_t.start()

    row = lax.broadcasted_iota(jnp.int32, (48, PER * ROWS), 0)
    col = lax.broadcasted_iota(jnp.int32, (48, PER * ROWS), 1)
    pick = (col == (row % 16) * 24 + (row // 16) * 8).astype(jnp.bfloat16)
    sample = lax.broadcasted_iota(jnp.int32, (TL, TL), 0)
    lag = lax.broadcasted_iota(jnp.int32, (TL, TL), 1)
    later = (sample >= lag).astype(jnp.bfloat16)
    earlier = (sample < lag).astype(jnp.bfloat16)
    last = lax.broadcasted_iota(jnp.int32, (8, 128), 0) == 7
    odd = jnp.where(lax.broadcasted_iota(jnp.int32, (8, 128), 1) % 2 == 0, 1.0, -1.0)

    def halo_copy(g):
        return pltpu.make_async_remote_copy(
            src_ref=halo_send.at[g], dst_ref=halo_recv.at[g],
            send_sem=halo_send_sem.at[g], recv_sem=halo_recv_sem.at[g],
            device_id={"sta": below}, device_id_type=MESH,
        )

    def main_part(g, slot):
        for k in range(PER):
            i = g * PER + k

            @pl.when(i > 0)
            def _():
                data_copy(i).wait_recv()

        block = recv[pl.ds(g * PER, PER)].reshape(PER * ROWS, TL)
        halo_send[g] = mm(pick, block).astype(jnp.bfloat16)
        halo_copy(g).start()
        for n in range(4):
            columns = pl.ds(n * 256, 256)
            parts[slot, :, columns] = mm(block, fwd_ref[:, columns])
        squares = jnp.square(block.astype(jnp.float32)).reshape(16, 3, 8, TL)
        squares = (squares[:, 0] + squares[:, 1] + squares[:, 2]).reshape(128, TL)
        high, low = split(squares)
        part_energy[slot, 0] = mm(high, later) + mm(low, later)
        part_energy[slot, 1] = mm(high, earlier) + mm(low, earlier)

    def halo_part(g, slot):
        halo_copy(g).wait_recv()
        block = jnp.where(z == depth - 1, jnp.zeros((48, TL), jnp.bfloat16), halo_recv[g])
        found = mm(block, fwd_ref[...])
        for n in range(8):
            halo_spec[n, 0:48, :] = found[:, n * 128:(n + 1) * 128]
        squares = jnp.square(block.astype(jnp.float32))
        high, low = split(squares[0:16] + squares[16:32] + squares[32:48])
        energy = mm(high, earlier) + mm(low, earlier)
        for n in range(4):
            halo_spec[n, 48:64, :] = energy[:, n * 128:(n + 1) * 128]

        def station(s, carry):
            for c in range(3):
                base = pl.multiple_of(s * 24 + c * 8, 8)
                halves = []
                for n in range(8):
                    now = parts[slot, pl.ds(base, 8), pl.ds(n * 128, 128)]
                    beyond = halo_spec[n, pl.ds(c * 16 + s, 8, stride=0), :]
                    following = jnp.where(last, beyond, pltpu.roll(now, 7, 0))
                    halves.append(now + odd * following)
                real = jnp.concatenate(halves[:4], axis=1)
                imag = jnp.concatenate(halves[4:], axis=1)
                spec[(g * 16 + s) * 3 + c] = jnp.concatenate([real, imag], axis=0).astype(jnp.bfloat16)
            base = pl.multiple_of(s * 8, 8)
            for n in range(4):
                columns = pl.ds(n * 128, 128)
                early = part_energy[slot, 1, pl.ds(base, 8), columns]
                beyond = halo_spec[n, pl.ds(48 + s, 8, stride=0), :]
                early = jnp.where(last, beyond, pltpu.roll(early, 7, 0))
                total = part_energy[slot, 0, pl.ds(base, 8), columns] + early
                rs[g * 16 + s, :, columns] = lax.rsqrt(total / SCALE + EPSILON)
            return carry

        lax.fori_loop(0, 16, station, 0)
        out_copies(g)[0].start()
        out_copies(g)[1].start()

    def out_copies(g):
        a = pl.ds(g * 48, 48)
        b = pl.ds(g * 16, 16)
        return (
            pltpu.make_async_copy(spec.at[a], spec_out.at[a], local_sem.at[2 + g]),
            pltpu.make_async_copy(rs.at[b], rs_out.at[b], local_sem.at[2 + GROUPS + g]),
        )

    main_part(0, 0)

    def turn(g, carry):
        main_part(g, lax.rem(g, 2))
        halo_part(g - 1, lax.rem(g - 1, 2))
        return carry

    lax.fori_loop(1, GROUPS, turn, 0)
    halo_part(GROUPS - 1, (GROUPS - 1) % 2)

    def finish(i, carry):
        data_copy(i).wait_send()
        return carry

    lax.fori_loop(1, count, finish, 0)

    def finish_group(g, carry):
        halo_copy(g).wait_send()
        for copy in out_copies(g):
            copy.wait()
        return carry

    lax.fori_loop(0, GROUPS, finish_group, 0)
    out_t.wait()


def exchange_call(mesh, rec, ask, templates, forward):
    count, depth = mesh.shape["tmpl"], mesh.shape["sta"]
    vmem = pl.BlockSpec(memory_space=pltpu.VMEM)
    hbm = pl.BlockSpec(memory_space=pl.ANY)
    f32, bf16 = jnp.float32, jnp.bfloat16
    slots = count * FETCH
    return pl.pallas_call(
        functools.partial(exchange_kernel, count, depth),
        out_shape=[
            jax.ShapeDtypeStruct((slots * 3, 16, TL), bf16),
            jax.ShapeDtypeStruct((slots, 8, TL), f32),
            jax.ShapeDtypeStruct((512 * 32, 128), f32),
        ],
        in_specs=[vmem] * 4,
        out_specs=[hbm] * 3,
        scratch_shapes=[
            pltpu.VMEM((4, 768, 128), f32),
            pltpu.VMEM((count, 1, 128), jnp.int32),
            pltpu.SMEM((count, 1, 128), jnp.int32),
            pltpu.VMEM((count, ROWS, TL), bf16),
            pltpu.VMEM((count, ROWS, TL), bf16),
            pltpu.VMEM((GROUPS, 48, TL), bf16),
            pltpu.VMEM((GROUPS, 48, TL), bf16),
            pltpu.VMEM((2, PER * ROWS, NBINS), f32),
            pltpu.VMEM((2, 2, 128, TL), f32),
            pltpu.VMEM((8, 64, 128), f32),
            pltpu.VMEM((slots * 3, 16, TL), bf16),
            pltpu.VMEM((slots, 8, TL), f32),
            pltpu.VMEM((512 * 32, 128), f32),
            pltpu.SemaphoreType.DMA((count,)),
            pltpu.SemaphoreType.DMA((count,)),
            pltpu.SemaphoreType.DMA((count,)),
            pltpu.SemaphoreType.DMA((count,)),
            pltpu.SemaphoreType.DMA((GROUPS,)),
            pltpu.SemaphoreType.DMA((GROUPS,)),
            pltpu.SemaphoreType.DMA((2 + 2 * GROUPS,)),
        ],
        compiler_params=pltpu.CompilerParams(
            collective_id=0, has_side_effects=True, vmem_limit_bytes=60 * 2**20
        ),
        name="exchange",
    )(rec, ask, templates, forward)


def pair_kernel(slot_ref, tmpl_ref, off_ref, live_ref, spec_ref, rs_ref, t_ref, inv_ref, pt_ref,
                out_ref, head_ref, acc, x0, x1, y0, y1):
    live = live_ref[0]
    nb = (live + PB - 1) // PB
    acc[...] = jnp.zeros_like(acc)
    y0[...] = jnp.zeros_like(y0)
    y1[...] = jnp.zeros_like(y1)
    lane = lax.broadcasted_iota(jnp.int32, (8, 128), 1)

    first = lane == 0

    def cross(block, x):
        for i in range(0, PB, 2):
            qs = [jnp.minimum(block * PB + i + k, 511) for k in range(2)]
            ss = [slot_ref[q] * 3 for q in qs]
            for g in range(4):
                rr, mm = [], []
                for q, s3 in zip(qs, ss):
                    t = t_ref[q, g]
                    R = M = None
                    for c in range(3):
                        b = spec_ref[s3 + c, :, pl.ds(g * 128, 128)].astype(jnp.float32)
                        br, bm = b[:8], b[8:]
                        ar = jnp.broadcast_to(t[c:c + 1], (8, 128))
                        am = jnp.broadcast_to(t[c + 3:c + 4], (8, 128))
                        cr = ar
                        if g == 0:
                            cr = jnp.where(first, am, ar)
                            am = jnp.where(first, 0.0, am)
                        r = ar * br + am * bm
                        m = cr * bm - am * br
                        R = r if R is None else R + r
                        M = m if M is None else M + m
                    rr.append(R)
                    mm.append(M)
                x[pl.ds(i * 8, 16), pl.ds(g * 128, 128)] = jnp.concatenate(rr, axis=0).astype(jnp.bfloat16)
                x[pl.ds(i * 8, 16), pl.ds(512 + g * 128, 128)] = jnp.concatenate(mm, axis=0).astype(jnp.bfloat16)

    def post(block, y):
        for i in range(PB):
            q = block * PB + i
            qc = jnp.clip(q, 0, 511)
            ok = (q >= 0) & (q < live)
            s = slot_ref[qc]
            j = jnp.where(ok, tmpl_ref[qc], 32)
            o = off_ref[qc]
            fine = o % 128
            low = lane < 128 - fine
            v = y[pl.ds(i * 8, 8), :] * rs_ref[s]
            turned = [pltpu.roll(v[:, g * 128:(g + 1) * 128], 128 - fine, 1) for g in range(4)]
            parts = [jnp.where(low, 0.0, turned[0])]
            for g in range(3):
                parts.append(jnp.where(low, turned[g], turned[g + 1]))
            parts.append(jnp.where(low, turned[3], 0.0))
            base = pl.multiple_of(j * 64 + 24 - 8 * (o // 128), 8)
            acc[pl.ds(base, 40), :] += jnp.concatenate(parts, axis=0)

    def dot(x, y):
        y[...] = jnp.dot(x[...], inv_ref[...], preferred_element_type=jnp.float32)

    def body(b2, _):
        b = b2 * 2
        post(b - 2, y0)
        dot(x1, y1)
        cross(b, x0)
        post(b - 1, y1)
        dot(x0, y0)
        cross(b + 1, x1)
        return 0
    x1[...] = jnp.zeros_like(x1)
    lax.fori_loop(0, (nb + 2 + 1) // 2, body, 0)

    same = (pt_ref[...] == lax.broadcasted_iota(jnp.int32, (32, 512), 0)) & (
        lax.broadcasted_iota(jnp.int32, (32, 512), 1) < live)
    counts = jnp.sum(same.astype(jnp.float32), axis=1, keepdims=True)
    scale = jnp.sqrt(1536.0 / counts)
    for g in range(4):
        lanes = pl.ds(g * 128, 128)
        head_ref[:, lanes] = acc[pl.ds(g * 8, 32, stride=64), :] * scale
        for h in range(8):
            v = acc[pl.ds(32 + g * 8 + h, 32, stride=64), :]
            if h < 7:
                v = v + acc[pl.ds(g * 8 + h + 1, 32, stride=64), :]
            out_ref[h, :, lanes] = v * scale


def pair_call(slot, tmpl, off, live, spec, rs, t, inverse, pt):
    smem = pl.BlockSpec(memory_space=pltpu.SMEM)
    vmem = pl.BlockSpec(memory_space=pltpu.VMEM)
    return pl.pallas_call(
        pair_kernel,
        out_shape=[
            jax.ShapeDtypeStruct((8, T_DEV, TL), jnp.float32),
            jax.ShapeDtypeStruct((T_DEV, TL), jnp.float32),
        ],
        in_specs=[smem] * 4 + [vmem] * 5,
        out_specs=[vmem] * 2,
        scratch_shapes=[
            pltpu.VMEM((33 * 64, 128), jnp.float32),
            pltpu.VMEM((PB * 8, NBINS), jnp.bfloat16),
            pltpu.VMEM((PB * 8, NBINS), jnp.bfloat16),
            pltpu.VMEM((PB * 8, TL), jnp.float32),
            pltpu.VMEM((PB * 8, TL), jnp.float32),
        ],
        compiler_params=pltpu.CompilerParams(vmem_limit_bytes=60 * 2**20),
        name="pairs",
    )(slot, tmpl, off, live, spec, rs, t, inverse, pt)


def shards(mesh, records, templates, requests, pair_slot, pair_template, pair_offset, live_pairs):
    count, depth = mesh.shape["tmpl"], mesh.shape["sta"]
    rec = jnp.transpose(records, (0, 2, 1, 3)).reshape(24, 32, TL)
    ask = jnp.pad(requests.reshape(count, 1, FETCH), ((0, 0), (0, 0), (0, 128 - FETCH)))
    spec, rs, temps = exchange_call(
        mesh, rec, ask, jnp.transpose(templates, (1, 0, 2)), jnp.asarray(FORWARD)
    )
    me = lax.axis_index("tmpl")
    slot = ((pair_slot // FETCH - me) % count) * FETCH + pair_slot % FETCH
    out, head = pair_call(
        slot, pair_template, pair_offset, live_pairs, spec, rs, temps.reshape(512, 4, 8, 128),
        jnp.asarray(INVERSE), pair_template.reshape(1, 512),
    )
    head = lax.ppermute(head, "sta", [(i, i - 1) for i in range(1, depth)])
    return out.at[7].add(head)


def solution(mesh):
    in_specs = (
        P("sta", "tmpl", None, None),
        P("tmpl", None, None),
        P("tmpl", None, None),
        P("tmpl"),
        P("tmpl"),
        P("tmpl"),
        P("tmpl"),
    )
    return jax.shard_map(
        functools.partial(shards, mesh), mesh=mesh, in_specs=in_specs,
        out_specs=P("sta", "tmpl", None), check_vma=False,
    )
```

time: 595 us -> 107 us (0.18)
  the two profiles are of different devices: /device:TPU:104 before, /device:TPU:30 now
where the time goes in v1:
time: 107 us
  Pallas kernels  95.4 us (89%)
  waiting for transfers between devices  5.07 us (5%)
  other arithmetic  2.77 us (3%)
  local copies, waits for them, and re-layouts  1.38 us (1%)
  starting transfers between devices  1.28 us (1%)
    pallas_call x1, Pallas kernels, exchange_call(): pl.pallas_call(functools.partial(exchange_kernel, count, depth), out_shap...  71.6 us
    pallas_call x1, Pallas kernels, pair_call(): pl.pallas_call(pair_kernel, out_shape=[jax.ShapeDtypeStruct((8, T_DEV, TL...  23.8 us
    ppermute x1, waiting for transfers between devices, shards(): head = lax.ppermute(head, 'sta', [(i, i - 1) for i in range(1, depth)])  5.07 us
  transfers between devices with their start and end apart: 1, of which 1 were waited for; matrix products, arithmetic and copies ran while one was open for 0% of the time, Pallas kernels for 0%

profile of v1, /device:TPU:30, one launch (start us, length us, event | category | flops | bytes accessed | tf_op | source)
XLA Modules:
  0.0 106.6 jit_solution(2756802705085214106)
XLA Ops:
  0.7 0.8 copy.10
  1.4 1.3 %fusion.4.slot_ref = s32[512]{0:T(512)} fusion(s32[512]{0:T(512)} %param.14, s32[]{:T(128)S(6)} %axis_index.15), kind=kLoop, calls=%fused_computation.13 | loop fusion | flops 16896 | bytes 4100 | tf_op jit(solution)/shard_map/add | solution.py:430
  2.7 0.6 pad.6.ask_ref
  3.3 71.6 %exchange.1 = (bf16[384,16,512]{2,1,0:T(8,128)(2,1)}, f32[128,8,512]{2,1,0:T(8,128)}, f32[16384,128]{1,0:T(8,128)}) custom-call(bf16[24,32,512]{2,1,0:T(8,128)(2,1)} %bitcast.13, s32[32,1,128]{2,1,0:T(1,128)} %pad.6.ask_ref, bf16[3,512,512]{2,1,0:T(8,128)(2,1)} %bitcast.12, bf16[512,1024]{1,0:T(8,128)(2,1)} %constant.79.clone.fwd_ref), custom_call_target="tpu_custom_call" | custom-call | tf_op jit(solution)/shard_map/exchange/pallas_call | solution.py:275
  74.9 23.8 %pairs.1 = (f32[8,32,512]{2,1,0:T(8,128)}, f32[32,512]{1,0:T(8,128)}) custom-call(s32[512]{0:T(512)} %fusion.4.slot_ref, s32[512]{0:T(512)} %tmpl_ref.1, s32[512]{0:T(512)} %off_ref.1, s32[1]{0:T(128)S(6)} %copy.12.live_ref, bf16[384,16,512]{2,1,0:T(8,128)(2,1)} %get-tuple-element.22.spec_ref, f32[128,8,512]{2,1,0:T(8,128)} %get-tuple-element.23.rs_ref, ...), custom_call_target="tpu_custom_call" | custom-call | tf_op jit(solution)/shard_map/pairs/pallas_call | solution.py:402
  98.7 1.3 %collective-permute-start = (f32[32,512]{1,0:T(8,128)}, f32[32,512]{1,0:T(8,128)S(1)}, u32[]{:S(2)}, u32[]{:S(2)}) collective-permute-start(f32[32,512]{1,0:T(8,128)} %get-tuple-element.26), channel_id=1, source_target_pairs={{1,0},{2,1},{3,2},{4,3},{5,4},{6,5},{7,6},{9,8},{10,9},{11,10},{12... | collective-permute-start | bytes 196616 | tf_op jit(solution)/shard_map/ppermute | solution.py:435
  100.0 5.1 %collective-permute-done = f32[32,512]{1,0:T(8,128)S(1)} collective-permute-done((f32[32,512]{1,0:T(8,128)}, f32[32,512]{1,0:T(8,128)S(1)}, u32[]{:S(2)}, u32[]{:S(2)}) %collective-permute-start) | collective-permute-done | bytes 65568 | tf_op jit(solution)/shard_map/ppermute | solution.py:435
  105.1 1.5 %fusion = f32[8,32,512]{2,1,0:T(8,128)} fusion(f32[8,32,512]{2,1,0:T(8,128)} %get-tuple-element.25, f32[32,512]{1,0:T(8,128)S(1)} %collective-permute-done), kind=kLoop, calls=%fused_computation.1 | loop fusion | flops 16384 | bytes 196608 | tf_op jit(solution)/shard_map/scatter-add | solution.py:436
Async XLA Ops:
  98.7 6.4 %collective-permute-start = (f32[32,512]{1,0:T(8,128)}, f32[32,512]{1,0:T(8,128)S(1)}, u32[]{:S(2)}, u32[]{:S(2)}) collective-permute-start(f32[32,512]{1,0:T(8,128)} %get-tuple-element.26), channel_id=1, source_target_pairs={{1,0},{2,1},{3,2},{4,3},{5,4},{6,5},{7,6},{9,8},{10,9},{11,10},{12... | collective-permute-start | bytes 196616 | tf_op jit(solution)/shard_map/ppermute | solution.py:435

commit v2 on v1

--- a/solution.py
+++ b/solution.py
@@ -16,6 +16,8 @@
 EPSILON = 1e-05
 MESH = pl.DeviceIdType.MESH
 PB = 16
+PAIRS = 512
+PLACES = 1024
 
 
 def dft_tables():
@@ -49,22 +51,103 @@
     return jnp.dot(left, right, preferred_element_type=jnp.float32)
 
 
+def cross_terms(lane, group, template, station):
+    real = imag = None
+    for c in range(3):
+        rows = station(c).astype(jnp.float32)
+        br, bm = rows[:8], rows[8:]
+        ar = jnp.broadcast_to(template[c:c + 1], (8, 128))
+        am = jnp.broadcast_to(template[c + 3:c + 4], (8, 128))
+        cr = ar
+        if group == 0:
+            cr = jnp.where(lane == 0, am, ar)
+            am = jnp.where(lane == 0, 0.0, am)
+        r = ar * br + am * bm
+        m = cr * bm - am * br
+        real = r if real is None else real + r
+        imag = m if imag is None else imag + m
+    return real, imag
+
+
+def two_pairs(lane, x, i, templates, stations):
+    for g in range(4):
+        terms = [cross_terms(lane, g, t(g), functools.partial(s, g)) for t, s in zip(templates, stations)]
+        for half in range(2):
+            rows = jnp.concatenate([t[half] for t in terms], axis=0).astype(jnp.bfloat16)
+            x[pl.ds(i * 8, 16), pl.ds(half * TL + g * 128, 128)] = rows
+
+
+def place_kernel(slot_ref, live_s, order):
+    f32, bf16 = jnp.float32, jnp.bfloat16
+    live = live_s[0]
+    me = lax.axis_index("tmpl")
+    y = me // 8
+    pair_row = lax.broadcasted_iota(jnp.int32, (PAIRS, PAIRS), 1)
+    pair_col = lax.broadcasted_iota(jnp.int32, (PAIRS, PAIRS), 0)
+    source = slot_ref[...] // FETCH
+    key_row = lax.rem(source + me, 2) * 4 + lax.rem(source // 8 - y + 4, 4)
+    key_row = jnp.where(pair_row[:1] < live, key_row, GROUPS).astype(f32)
+    ones = jnp.ones((PAIRS, 128), bf16)
+    key_col = mm(jnp.where(pair_row == pair_col, key_row, 0.0).astype(bf16), ones)
+    wide = jnp.concatenate([key_col] * 4, axis=1)
+    ahead_of = (key_row < wide) | ((key_row == wide) & (pair_row < pair_col))
+    rank_col = mm(ahead_of.astype(f32).astype(bf16), ones)
+    group_row = lax.broadcasted_iota(jnp.int32, (PAIRS, 128), 1).astype(f32)
+    below_count = mm(jnp.ones((8, PAIRS), bf16), (key_col < group_row).astype(f32).astype(bf16))[:1]
+    gap = jnp.maximum(32.0 * (2.0 * group_row[:1] - 1.0), 0.0) - below_count
+    gap = jnp.where((group_row <= key_col) & (group_row < GROUPS), gap, 0.0)
+    place_col = rank_col + jnp.maximum(jnp.max(gap, axis=1, keepdims=True), 0.0)
+    place_col = jnp.where(key_col < GROUPS, place_col, 2.0 * PLACES)
+    number = lax.broadcasted_iota(jnp.int32, (8, PAIRS), 1)
+    row_of = lax.broadcasted_iota(jnp.int32, (8, PAIRS), 0)
+    digits = jnp.where(row_of == 0, number // 16, jnp.where(row_of == 1, lax.rem(number, 16), 1))
+    digits = digits.astype(f32).astype(bf16)
+    for n in range(PLACES // 128):
+        here = (place_col == group_row + n * 128.0).astype(f32).astype(bf16)
+        found = mm(digits, here)
+        order[:, pl.ds(n * 128, 128)] = jnp.where(
+            found[2:3] > 0.5, found[0:1] * 16.0 + found[1:2], -1.0
+        ).astype(jnp.int32)
+
+
+def place_call(slot, live):
+    vmem = pl.BlockSpec(memory_space=pltpu.VMEM)
+    return pl.pallas_call(
+        place_kernel,
+        out_shape=jax.ShapeDtypeStruct((1, PLACES), jnp.int32),
+        in_specs=[vmem, pl.BlockSpec(memory_space=pltpu.SMEM)],
+        out_specs=vmem,
+        name="places",
+    )(slot.reshape(1, PAIRS), live)
+
+
 def exchange_kernel(
-    count, depth, rec_ref, ask_ref, tmp_ref, fwd_ref, spec_out, rs_out, t_out,
+    count, depth, order_s, slot_s, rec_ref, ask_ref, tmp_ref, fwd_ref, inv_ref,
+    spec_out, rs_out, t_out, done_out,
     rec32, asked, wanted, send, recv, halo_send, halo_recv, parts, part_energy, halo_spec,
-    spec, rs, temps,
-    ask_send_sem, ask_recv_sem, send_sem, recv_sem, halo_send_sem, halo_recv_sem, local_sem,
+    spec, rs, temps, x0, x1, done,
+    ask_send_sem, ask_recv_sem, send_sem, recv_sem, halo_send_sem, halo_recv_sem, local_sem, done_sem, spec_sem, rs_sem,
 ):
     me = lax.axis_index("tmpl")
     z = lax.axis_index("sta")
     above = lax.rem(z + 1, depth)
     below = lax.rem(z + depth - 1, depth)
 
+    y, x, core = me // 8, lax.rem(me // 2, 4), lax.rem(me, 2)
+
+    def place(up, right, other):
+        return lax.rem(y + up + 8, 4) * 8 + lax.rem(x + right + 8, 4) * 2 + lax.rem(core + other, 2)
+
+    def steps(i):
+        return lax.rem(i // 4, 4), lax.rem(i, 4), i // 16
+
     def ahead(i):
-        return lax.rem(me + i, count)
+        up, right, other = steps(i)
+        return place(up, right, other)
 
     def behind(i):
-        return lax.rem(me + count - i, count)
+        up, right, other = steps(i)
+        return place(-up, -right, other)
 
     barrier = pltpu.get_barrier_semaphore()
 
@@ -157,6 +240,45 @@
     out_t = pltpu.make_async_copy(temps, t_out, local_sem.at[1])
     out_t.start()
 
+    x1[...] = jnp.zeros_like(x1)
+    lane8 = lax.broadcasted_iota(jnp.int32, (8, 128), 1)
+
+    def pair_at(place):
+        return jnp.maximum(order_s[0, jnp.maximum(place, 0)], 0)
+
+    def cross_block(block, x):
+        for i in range(0, PB, 2):
+            templates, stations = [], []
+            for k in range(2):
+                q = pair_at(block * PB + i + k)
+                base = slot_s[q] * 3
+                templates.append(
+                    lambda g, q=q: temps[pl.ds(q * 32 + g * 8, 8), :]
+                )
+                stations.append(lambda g, c, base=base: spec[base + c, :, pl.ds(g * 128, 128)])
+            two_pairs(lane8, x, i, templates, stations)
+
+    def invert_block(block, x):
+        lagged = mm(x[...], inv_ref[...])
+        for i in range(PB):
+            place = block * PB + i
+            done[place + PB] = lagged[i * 8:i * 8 + 8] * rs[slot_s[pair_at(place)]]
+
+    def done_copy(n):
+        rows = pl.ds(n * 32, 32)
+        return pltpu.make_async_copy(done.at[rows], done_out.at[rows], done_sem.at[n])
+
+    def pair_turn(n, carry):
+        invert_block(2 * n - 1, x1)
+        cross_block(2 * n, x0)
+        invert_block(2 * n, x0)
+        cross_block(2 * n + 1, x1)
+        done_copy(n).start()
+        return carry
+
+    def stage(k):
+        lax.fori_loop(jnp.maximum(2 * k - 1, 0), 2 * k + 1, pair_turn, 0)
+
     row = lax.broadcasted_iota(jnp.int32, (48, PER * ROWS), 0)
     col = lax.broadcasted_iota(jnp.int32, (48, PER * ROWS), 1)
     pick = (col == (row % 16) * 24 + (row // 16) * 8).astype(jnp.bfloat16)
@@ -194,6 +316,9 @@
         part_energy[slot, 0] = mm(high, later) + mm(low, later)
         part_energy[slot, 1] = mm(high, earlier) + mm(low, earlier)
 
+    def station_at(g, s):
+        return ahead(g * PER + s // FETCH) * FETCH + lax.rem(s, FETCH)
+
     def halo_part(g, slot):
         halo_copy(g).wait_recv()
         block = jnp.where(z == depth - 1, jnp.zeros((48, TL), jnp.bfloat16), halo_recv[g])
@@ -217,7 +342,7 @@
                     halves.append(now + odd * following)
                 real = jnp.concatenate(halves[:4], axis=1)
                 imag = jnp.concatenate(halves[4:], axis=1)
-                spec[(g * 16 + s) * 3 + c] = jnp.concatenate([real, imag], axis=0).astype(jnp.bfloat16)
+                spec[station_at(g, s) * 3 + c] = jnp.concatenate([real, imag], axis=0).astype(jnp.bfloat16)
             base = pl.multiple_of(s * 8, 8)
             for n in range(4):
                 columns = pl.ds(n * 128, 128)
@@ -225,30 +350,40 @@
                 beyond = halo_spec[n, pl.ds(48 + s, 8, stride=0), :]
                 early = jnp.where(last, beyond, pltpu.roll(early, 7, 0))
                 total = part_energy[slot, 0, pl.ds(base, 8), columns] + early
-                rs[g * 16 + s, :, columns] = lax.rsqrt(total / SCALE + EPSILON)
+                rs[station_at(g, s), :, columns] = lax.rsqrt(total / SCALE + EPSILON)
             return carry
 
         lax.fori_loop(0, 16, station, 0)
-        out_copies(g)[0].start()
-        out_copies(g)[1].start()
-
-    def out_copies(g):
-        a = pl.ds(g * 48, 48)
-        b = pl.ds(g * 16, 16)
-        return (
-            pltpu.make_async_copy(spec.at[a], spec_out.at[a], local_sem.at[2 + g]),
-            pltpu.make_async_copy(rs.at[b], rs_out.at[b], local_sem.at[2 + GROUPS + g]),
-        )
+
+        def leave(k, carry):
+            spec_copy(g * PER + k).start()
+            rs_copy(g * PER + k).start()
+            return carry
+
+        lax.fori_loop(0, PER, leave, 0)
+
+    def spec_copy(i):
+        rows = pl.ds(ahead(i) * (FETCH * 3), FETCH * 3)
+        return pltpu.make_async_copy(spec.at[rows], spec_out.at[rows], spec_sem.at[i])
+
+    def rs_copy(i):
+        rows = pl.ds(ahead(i) * FETCH, FETCH)
+        return pltpu.make_async_copy(rs.at[rows], rs_out.at[rows], rs_sem.at[i])
 
     main_part(0, 0)
 
     def turn(g, carry):
         main_part(g, lax.rem(g, 2))
         halo_part(g - 1, lax.rem(g - 1, 2))
+        stage(g - 1)
         return carry
 
     lax.fori_loop(1, GROUPS, turn, 0)
     halo_part(GROUPS - 1, (GROUPS - 1) % 2)
+    lax.fori_loop(2 * GROUPS - 3, PAIRS // 32, pair_turn, 0)
+    invert_block(PAIRS // PB - 1, x1)
+    rest = pltpu.make_async_copy(done.at[pl.ds(PAIRS, PB)], done_out.at[pl.ds(PAIRS, PB)], local_sem.at[3])
+    rest.start()
 
     def finish(i, carry):
         data_copy(i).wait_send()
@@ -258,18 +393,29 @@
 
     def finish_group(g, carry):
         halo_copy(g).wait_send()
-        for copy in out_copies(g):
-            copy.wait()
+        return carry
+
+    def finish_source(i, carry):
+        spec_copy(i).wait()
+        rs_copy(i).wait()
+        return carry
+
+    def finish_places(n, carry):
+        done_copy(n).wait()
         return carry
 
     lax.fori_loop(0, GROUPS, finish_group, 0)
+    lax.fori_loop(0, count, finish_source, 0)
+    lax.fori_loop(0, PAIRS // 32, finish_places, 0)
+    rest.wait()
     out_t.wait()
 
 
-def exchange_call(mesh, rec, ask, templates, forward):
+def exchange_call(mesh, order, slot, rec, ask, templates, forward, inverse):
     count, depth = mesh.shape["tmpl"], mesh.shape["sta"]
     vmem = pl.BlockSpec(memory_space=pltpu.VMEM)
     hbm = pl.BlockSpec(memory_space=pl.ANY)
+    smem = pl.BlockSpec(memory_space=pltpu.SMEM)
     f32, bf16 = jnp.float32, jnp.bfloat16
     slots = count * FETCH
     return pl.pallas_call(
@@ -278,9 +424,10 @@
             jax.ShapeDtypeStruct((slots * 3, 16, TL), bf16),
             jax.ShapeDtypeStruct((slots, 8, TL), f32),
             jax.ShapeDtypeStruct((512 * 32, 128), f32),
+            jax.ShapeDtypeStruct((PAIRS + PB, 8, TL), f32),
         ],
-        in_specs=[vmem] * 4,
-        out_specs=[hbm] * 3,
+        in_specs=[smem] * 2 + [vmem] * 5,
+        out_specs=[hbm] * 4,
         scratch_shapes=[
             pltpu.VMEM((4, 768, 128), f32),
             pltpu.VMEM((count, 1, 128), jnp.int32),
@@ -295,142 +442,165 @@
             pltpu.VMEM((slots * 3, 16, TL), bf16),
             pltpu.VMEM((slots, 8, TL), f32),
             pltpu.VMEM((512 * 32, 128), f32),
+            pltpu.VMEM((PB * 8, NBINS), bf16),
+            pltpu.VMEM((PB * 8, NBINS), bf16),
+            pltpu.VMEM((PAIRS + PB, 8, TL), f32),
             pltpu.SemaphoreType.DMA((count,)),
             pltpu.SemaphoreType.DMA((count,)),
             pltpu.SemaphoreType.DMA((count,)),
             pltpu.SemaphoreType.DMA((count,)),
             pltpu.SemaphoreType.DMA((GROUPS,)),
             pltpu.SemaphoreType.DMA((GROUPS,)),
-            pltpu.SemaphoreType.DMA((2 + 2 * GROUPS,)),
+            pltpu.SemaphoreType.DMA((4,)),
+            pltpu.SemaphoreType.DMA((PAIRS // 32,)),
+            pltpu.SemaphoreType.DMA((count,)),
+            pltpu.SemaphoreType.DMA((count,)),
         ],
         compiler_params=pltpu.CompilerParams(
             collective_id=0, has_side_effects=True, vmem_limit_bytes=60 * 2**20
         ),
         name="exchange",
-    )(rec, ask, templates, forward)
-
-
-def pair_kernel(slot_ref, tmpl_ref, off_ref, live_ref, spec_ref, rs_ref, t_ref, inv_ref, pt_ref,
-                out_ref, head_ref, acc, x0, x1, y0, y1):
+    )(order, slot, rec, ask, templates, forward, inverse)
+
+
+CHUNKS = 8
+
+
+def pair_kernel(
+    order_ref, slot_ref, tmpl_ref, off_ref, live_ref, inv_ref, pt_ref, spec_in, rs_in, t_in, done_in,
+    out_ref, head_ref,
+    acc, done, x, y, spec, rs, temps, done_sem, spec_sem, rs_sem, t_sem,
+):
     live = live_ref[0]
-    nb = (live + PB - 1) // PB
+    lane = lax.broadcasted_iota(jnp.int32, (8, 128), 1)
+
+    def chunk(n):
+        rows = pl.ds(n * (PAIRS // CHUNKS), PAIRS // CHUNKS)
+        return pltpu.make_async_copy(
+            done_in.at[pl.ds(n * (PAIRS // CHUNKS) + PB, PAIRS // CHUNKS)], done.at[rows], done_sem.at[n]
+        )
+
+    for n in range(CHUNKS):
+        chunk(n).start()
     acc[...] = jnp.zeros_like(acc)
-    y0[...] = jnp.zeros_like(y0)
-    y1[...] = jnp.zeros_like(y1)
-    lane = lax.broadcasted_iota(jnp.int32, (8, 128), 1)
-
-    first = lane == 0
-
-    def cross(block, x):
+
+    def add(place, row):
+        q = order_ref[0, place]
+        j = jnp.where(q >= 0, tmpl_ref[jnp.maximum(q, 0)], T_DEV)
+        o = off_ref[jnp.maximum(q, 0)]
+        coarse = lax.shift_right_logical(o, 7)
+        fine = o & 127
+        low = lane < 128 - fine
+        turned = [pltpu.roll(row[:, g * 128:(g + 1) * 128], 128 - fine, 1) for g in range(4)]
+        parts = [jnp.where(low, 0.0, turned[0])]
+        for g in range(3):
+            parts.append(jnp.where(low, turned[g], turned[g + 1]))
+        parts.append(jnp.where(low, turned[3], 0.0))
+        base = pl.multiple_of(j * 64 + 24 - 8 * coarse, 8)
+        acc[pl.ds(base, 40), :] += jnp.concatenate(parts, axis=0)
+
+    def add_some(b, carry):
+        for i in range(8):
+            add(b * 8 + i, done[b * 8 + i])
+        return carry
+
+    for n in range(CHUNKS):
+        chunk(n).wait()
+        lax.fori_loop(n * (PAIRS // CHUNKS // 8), (n + 1) * (PAIRS // CHUNKS // 8), add_some, 0)
+
+    def copies(q, i):
+        s = slot_ref[q]
+        return (
+            pltpu.make_async_copy(spec_in.at[pl.ds(s * 3, 3)], spec.at[i], spec_sem.at[i]),
+            pltpu.make_async_copy(rs_in.at[s], rs.at[i], rs_sem.at[i]),
+            pltpu.make_async_copy(t_in.at[pl.ds(pl.multiple_of(q * 32, 32), 32)], temps.at[i], t_sem.at[i]),
+        )
+
+    def late_block(first):
+        qs = [jnp.maximum(order_ref[0, first + i], 0) for i in range(PB)]
+        for i, q in enumerate(qs):
+            for copy in copies(q, i):
+                copy.start()
+        for i, q in enumerate(qs):
+            for copy in copies(q, i):
+                copy.wait()
         for i in range(0, PB, 2):
-            qs = [jnp.minimum(block * PB + i + k, 511) for k in range(2)]
-            ss = [slot_ref[q] * 3 for q in qs]
-            for g in range(4):
-                rr, mm = [], []
-                for q, s3 in zip(qs, ss):
-                    t = t_ref[q, g]
-                    R = M = None
-                    for c in range(3):
-                        b = spec_ref[s3 + c, :, pl.ds(g * 128, 128)].astype(jnp.float32)
-                        br, bm = b[:8], b[8:]
-                        ar = jnp.broadcast_to(t[c:c + 1], (8, 128))
-                        am = jnp.broadcast_to(t[c + 3:c + 4], (8, 128))
-                        cr = ar
-                        if g == 0:
-                            cr = jnp.where(first, am, ar)
-                            am = jnp.where(first, 0.0, am)
-                        r = ar * br + am * bm
-                        m = cr * bm - am * br
-                        R = r if R is None else R + r
-                        M = m if M is None else M + m
-                    rr.append(R)
-                    mm.append(M)
-                x[pl.ds(i * 8, 16), pl.ds(g * 128, 128)] = jnp.concatenate(rr, axis=0).astype(jnp.bfloat16)
-                x[pl.ds(i * 8, 16), pl.ds(512 + g * 128, 128)] = jnp.concatenate(mm, axis=0).astype(jnp.bfloat16)
-
-    def post(block, y):
+            two_pairs(
+                lane, x, i,
+                [lambda g, k=k: temps[k, pl.ds(g * 8, 8), :] for k in (i, i + 1)],
+                [lambda g, c, k=k: spec[k, c, :, pl.ds(g * 128, 128)] for k in (i, i + 1)],
+            )
+        y[...] = mm(x[...], inv_ref[...])
         for i in range(PB):
-            q = block * PB + i
-            qc = jnp.clip(q, 0, 511)
-            ok = (q >= 0) & (q < live)
-            s = slot_ref[qc]
-            j = jnp.where(ok, tmpl_ref[qc], 32)
-            o = off_ref[qc]
-            fine = o % 128
-            low = lane < 128 - fine
-            v = y[pl.ds(i * 8, 8), :] * rs_ref[s]
-            turned = [pltpu.roll(v[:, g * 128:(g + 1) * 128], 128 - fine, 1) for g in range(4)]
-            parts = [jnp.where(low, 0.0, turned[0])]
-            for g in range(3):
-                parts.append(jnp.where(low, turned[g], turned[g + 1]))
-            parts.append(jnp.where(low, turned[3], 0.0))
-            base = pl.multiple_of(j * 64 + 24 - 8 * (o // 128), 8)
-            acc[pl.ds(base, 40), :] += jnp.concatenate(parts, axis=0)
-
-    def dot(x, y):
-        y[...] = jnp.dot(x[...], inv_ref[...], preferred_element_type=jnp.float32)
-
-    def body(b2, _):
-        b = b2 * 2
-        post(b - 2, y0)
-        dot(x1, y1)
-        cross(b, x0)
-        post(b - 1, y1)
-        dot(x0, y0)
-        cross(b + 1, x1)
-        return 0
-    x1[...] = jnp.zeros_like(x1)
-    lax.fori_loop(0, (nb + 2 + 1) // 2, body, 0)
-
-    same = (pt_ref[...] == lax.broadcasted_iota(jnp.int32, (32, 512), 0)) & (
-        lax.broadcasted_iota(jnp.int32, (32, 512), 1) < live)
+            add(first + i, y[pl.ds(i * 8, 8), :] * rs[i])
+
+    def late(n, carry):
+        first = PAIRS + n * PB
+
+        @pl.when(order_ref[0, first] >= 0)
+        def _():
+            late_block(first)
+
+        return carry
+
+    @pl.when(order_ref[0, PAIRS] >= 0)
+    def _():
+        lax.fori_loop(0, (PLACES - PAIRS) // PB, late, 0)
+
+    same = (pt_ref[...] == lax.broadcasted_iota(jnp.int32, (T_DEV, PAIRS), 0)) & (
+        lax.broadcasted_iota(jnp.int32, (T_DEV, PAIRS), 1) < live
+    )
     counts = jnp.sum(same.astype(jnp.float32), axis=1, keepdims=True)
-    scale = jnp.sqrt(1536.0 / counts)
+    scale = jnp.sqrt(SCALE / counts)
     for g in range(4):
         lanes = pl.ds(g * 128, 128)
-        head_ref[:, lanes] = acc[pl.ds(g * 8, 32, stride=64), :] * scale
+        head_ref[:, lanes] = acc[pl.ds(g * 8, T_DEV, stride=64), :] * scale
         for h in range(8):
-            v = acc[pl.ds(32 + g * 8 + h, 32, stride=64), :]
+            v = acc[pl.ds(32 + g * 8 + h, T_DEV, stride=64), :]
             if h < 7:
-                v = v + acc[pl.ds(g * 8 + h + 1, 32, stride=64), :]
+                v = v + acc[pl.ds(g * 8 + h + 1, T_DEV, stride=64), :]
             out_ref[h, :, lanes] = v * scale
 
 
-def pair_call(slot, tmpl, off, live, spec, rs, t, inverse, pt):
+def pair_call(order, slot, tmpl, off, live, inverse, spec, rs, t, done):
     smem = pl.BlockSpec(memory_space=pltpu.SMEM)
     vmem = pl.BlockSpec(memory_space=pltpu.VMEM)
+    hbm = pl.BlockSpec(memory_space=pl.ANY)
+    f32, bf16 = jnp.float32, jnp.bfloat16
     return pl.pallas_call(
         pair_kernel,
-        out_shape=[
-            jax.ShapeDtypeStruct((8, T_DEV, TL), jnp.float32),
-            jax.ShapeDtypeStruct((T_DEV, TL), jnp.float32),
-        ],
-        in_specs=[smem] * 4 + [vmem] * 5,
+        out_shape=[jax.ShapeDtypeStruct((8, T_DEV, TL), f32), jax.ShapeDtypeStruct((T_DEV, TL), f32)],
+        in_specs=[smem] * 5 + [vmem] * 2 + [hbm] * 4,
         out_specs=[vmem] * 2,
         scratch_shapes=[
-            pltpu.VMEM((33 * 64, 128), jnp.float32),
-            pltpu.VMEM((PB * 8, NBINS), jnp.bfloat16),
-            pltpu.VMEM((PB * 8, NBINS), jnp.bfloat16),
-            pltpu.VMEM((PB * 8, TL), jnp.float32),
-            pltpu.VMEM((PB * 8, TL), jnp.float32),
+            pltpu.VMEM(((T_DEV + 1) * 64, 128), f32),
+            pltpu.VMEM((PAIRS, 8, TL), f32),
+            pltpu.VMEM((PB * 8, NBINS), bf16),
+            pltpu.VMEM((PB * 8, TL), f32),
+            pltpu.VMEM((PB, 3, 16, TL), bf16),
+            pltpu.VMEM((PB, 8, TL), f32),
+            pltpu.VMEM((PB, 32, 128), f32),
+            pltpu.SemaphoreType.DMA((CHUNKS,)),
+            pltpu.SemaphoreType.DMA((PB,)),
+            pltpu.SemaphoreType.DMA((PB,)),
+            pltpu.SemaphoreType.DMA((PB,)),
         ],
-        compiler_params=pltpu.CompilerParams(vmem_limit_bytes=60 * 2**20),
+        compiler_params=pltpu.CompilerParams(vmem_limit_bytes=40 * 2**20),
         name="pairs",
-    )(slot, tmpl, off, live, spec, rs, t, inverse, pt)
+    )(order, slot, tmpl, off, live, inverse, tmpl.reshape(1, PAIRS), spec, rs, t, done)
 
 
 def shards(mesh, records, templates, requests, pair_slot, pair_template, pair_offset, live_pairs):
     count, depth = mesh.shape["tmpl"], mesh.shape["sta"]
     rec = jnp.transpose(records, (0, 2, 1, 3)).reshape(24, 32, TL)
     ask = jnp.pad(requests.reshape(count, 1, FETCH), ((0, 0), (0, 0), (0, 128 - FETCH)))
-    spec, rs, temps = exchange_call(
-        mesh, rec, ask, jnp.transpose(templates, (1, 0, 2)), jnp.asarray(FORWARD)
+    order = place_call(pair_slot, live_pairs)
+    spec, rs, temps, done = exchange_call(
+        mesh, order, pair_slot, rec, ask, jnp.transpose(templates, (1, 0, 2)), jnp.asarray(FORWARD),
+        jnp.asarray(INVERSE),
     )
-    me = lax.axis_index("tmpl")
-    slot = ((pair_slot // FETCH - me) % count) * FETCH + pair_slot % FETCH
     out, head = pair_call(
-        slot, pair_template, pair_offset, live_pairs, spec, rs, temps.reshape(512, 4, 8, 128),
-        jnp.asarray(INVERSE), pair_template.reshape(1, 512),
+        order, pair_slot, pair_template, pair_offset, live_pairs, jnp.asarray(INVERSE), spec, rs, temps, done
     )
     head = lax.ppermute(head, "sta", [(i, i - 1) for i in range(1, depth)])
     return out.at[7].add(head)

time: 107 us -> 106 us (level)
  the two profiles are of different devices: /device:TPU:30 before, /device:TPU:7 now
where the time goes in v2:
time: 106 us
  Pallas kernels  88.6 us (84%)
  local copies, waits for them, and re-layouts  9.7 us (9%)
  waiting for transfers between devices  3.71 us (4%)
  other arithmetic  1.48 us (1%)
  starting transfers between devices  1.29 us (1%)
    pallas_call x1, Pallas kernels, exchange_call(): pl.pallas_call(functools.partial(exchange_kernel, count, depth), out_shap...  74.2 us
    pallas_call x1, Pallas kernels, pair_call(): pl.pallas_call(pair_kernel, out_shape=[jax.ShapeDtypeStruct((8, T_DEV, TL...  12.1 us
    unnamed x14, local copies, waits for them, and re-layouts  8.32 us
    ppermute x1, waiting for transfers between devices, shards(): head = lax.ppermute(head, 'sta', [(i, i - 1) for i in range(1, depth)])  3.71 us
    pallas_call x1, Pallas kernels, place_call(): pl.pallas_call(place_kernel, out_shape=jax.ShapeDtypeStruct((1, PLACES),...  2.37 us
  transfers between devices with their start and end apart: 1, of which 1 were waited for; matrix products, arithmetic and copies ran while one was open for 0% of the time, Pallas kernels for 0%

profile of v2, /device:TPU:7, one launch (start us, length us, event | category | flops | bytes accessed | tf_op | source)
XLA Modules:
  0.0 105.5 jit_solution(2374111491949490375)
XLA Ops:
  0.7 0.8 copy.10
  1.4 2.4 %places.1.order_s.order_ref = s32[1,1024]{1,0:T(1,128)} custom-call(s32[1,512]{1,0:T(1,128)} %bitcast.11, s32[1]{0:T(128)S(6)} %copy.12.live_s.live_ref), custom_call_target="tpu_custom_call" | custom-call | tf_op jit(solution)/shard_map/places/pallas_call | solution.py:115
  3.8 0.6 pad.6.ask_ref
  4.4 74.2 %exchange.1 = (bf16[384,16,512]{2,1,0:T(8,128)(2,1)}, f32[128,8,512]{2,1,0:T(8,128)}, f32[16384,128]{1,0:T(8,128)}, f32[528,8,512]{2,1,0:T(8,128)}) custom-call(s32[1,1024]{1,0:T(1,128)} %places.1.order_s.order_ref, s32[512]{0:T(512)} %slot_ref.1, bf16[24,32,512]{2,1,0:T(8,128)(2,1)} %bitcast.14, s32[32,1,128]{2,1,0:T(1,128)} %pad.6.ask_ref, ...), custom_call_target="tpu_custom_call" | custom-call | tf_op jit(solution)/shard_map/exchange/pallas_call | solution.py:421
  78.6 0.0 copy-start
  78.6 2.8 %copy-done = bf16[384,16,512]{2,1,0:T(8,128)(2,1)S(1)} copy-done((bf16[384,16,512]{2,1,0:T(8,128)(2,1)S(1)}, bf16[384,16,512]{2,1,0:T(8,128)(2,1)}, u32[]{:S(2)}) %copy-start) | copy-done | bytes 6291480
  81.4 0.0 copy-start.1
  81.4 1.2 %copy-done.1 = bf16[1024,512]{1,0:T(8,128)(2,1)S(1)} copy-done((bf16[1024,512]{1,0:T(8,128)(2,1)S(1)}, bf16[1024,512]{1,0:T(8,128)(2,1)}, u32[]{:S(2)}) %copy-start.1) | copy-done | bytes 1048600
  82.6 0.0 copy-start.2
  82.6 1.6 %copy-done.2 = f32[128,8,512]{2,1,0:T(8,128)S(1)} copy-done((f32[128,8,512]{2,1,0:T(8,128)S(1)}, f32[128,8,512]{2,1,0:T(8,128)}, u32[]{:S(2)}) %copy-start.2) | copy-done | bytes 2097176
  84.2 0.0 copy-start.3
  84.2 0.7 copy-done.3
  84.9 0.0 copy-start.4
  84.9 0.7 copy-done.4
  85.6 0.0 copy-start.5
  85.6 0.7 copy-done.5
  86.3 0.0 copy-start.6
  86.3 0.7 copy-done.6
  87.0 12.1 %pairs.1 = (f32[8,32,512]{2,1,0:T(8,128)}, f32[32,512]{1,0:T(8,128)S(1)}) custom-call(s32[1,1024]{1,0:T(1,128)S(1)} %copy-done.3, s32[512]{0:T(512)S(1)} %copy-done.4, s32[512]{0:T(512)S(1)} %copy-done.5, s32[512]{0:T(512)S(1)} %copy-done.6, s32[1]{0:T(128)S(6)} %copy.12.live_s.live_ref, bf16[1024,512]{1,0:T(8,128)(2,1)S(1)} %copy-done.1, ...), custom_call_target="tpu_custom_call" | custom-call | tf_op jit(solution)/shard_map/pairs/pallas_call | solution.py:570
  99.0 1.3 %collective-permute-start = (f32[32,512]{1,0:T(8,128)S(1)}, f32[32,512]{1,0:T(8,128)S(1)}, u32[]{:S(2)}, u32[]{:S(2)}) collective-permute-start(f32[32,512]{1,0:T(8,128)S(1)} %get-tuple-element.28), channel_id=1, source_target_pairs={{1,0},{2,1},{3,2},{4,3},{5,4},{6,5},{7,6},{9,8},{10,9},{11,10},{12... | collective-permute-start | bytes 196616 | tf_op jit(solution)/shard_map/ppermute | solution.py:605
  100.3 3.7 %collective-permute-done = f32[32,512]{1,0:T(8,128)S(1)} collective-permute-done((f32[32,512]{1,0:T(8,128)S(1)}, f32[32,512]{1,0:T(8,128)S(1)}, u32[]{:S(2)}, u32[]{:S(2)}) %collective-permute-start) | collective-permute-done | bytes 65568 | tf_op jit(solution)/shard_map/ppermute | solution.py:605
  104.0 1.5 %fusion = f32[8,32,512]{2,1,0:T(8,128)} fusion(f32[8,32,512]{2,1,0:T(8,128)} %get-tuple-element.27, f32[32,512]{1,0:T(8,128)S(1)} %collective-permute-done), kind=kLoop, calls=%fused_computation.1 | loop fusion | flops 16384 | bytes 196608 | tf_op jit(solution)/shard_map/scatter-add | solution.py:606
Async XLA Ops:
  78.6 2.8 %copy-start = (bf16[384,16,512]{2,1,0:T(8,128)(2,1)S(1)}, bf16[384,16,512]{2,1,0:T(8,128)(2,1)}, u32[]{:S(2)}) copy-start(bf16[384,16,512]{2,1,0:T(8,128)(2,1)} %get-tuple-element.23.spec_in) | copy-start | bytes 18874372
  81.4 1.2 %copy-start.1 = (bf16[1024,512]{1,0:T(8,128)(2,1)S(1)}, bf16[1024,512]{1,0:T(8,128)(2,1)}, u32[]{:S(2)}) copy-start(bf16[1024,512]{1,0:T(8,128)(2,1)} %constant.35.clone.inv_ref) | copy-start | bytes 3145732
  82.6 1.6 %copy-start.2 = (f32[128,8,512]{2,1,0:T(8,128)S(1)}, f32[128,8,512]{2,1,0:T(8,128)}, u32[]{:S(2)}) copy-start(f32[128,8,512]{2,1,0:T(8,128)} %get-tuple-element.24.rs_in) | copy-start | bytes 6291460
  84.2 0.7 copy-start.3
  84.9 0.7 copy-start.4
  85.6 0.7 copy-start.5
  86.3 0.7 copy-start.6
  99.0 5.0 %collective-permute-start = (f32[32,512]{1,0:T(8,128)S(1)}, f32[32,512]{1,0:T(8,128)S(1)}, u32[]{:S(2)}, u32[]{:S(2)}) collective-permute-start(f32[32,512]{1,0:T(8,128)S(1)} %get-tuple-element.28), channel_id=1, source_target_pairs={{1,0},{2,1},{3,2},{4,3},{5,4},{6,5},{7,6},{9,8},{10,9},{11,10},{12... | collective-permute-start | bytes 196616 | tf_op jit(solution)/shard_map/ppermute | solution.py:605

commit v3 on v2

--- a/solution.py
+++ b/solution.py
@@ -77,55 +77,11 @@
             x[pl.ds(i * 8, 16), pl.ds(half * TL + g * 128, 128)] = rows
 
 
-def place_kernel(slot_ref, live_s, order):
-    f32, bf16 = jnp.float32, jnp.bfloat16
-    live = live_s[0]
-    me = lax.axis_index("tmpl")
-    y = me // 8
-    pair_row = lax.broadcasted_iota(jnp.int32, (PAIRS, PAIRS), 1)
-    pair_col = lax.broadcasted_iota(jnp.int32, (PAIRS, PAIRS), 0)
-    source = slot_ref[...] // FETCH
-    key_row = lax.rem(source + me, 2) * 4 + lax.rem(source // 8 - y + 4, 4)
-    key_row = jnp.where(pair_row[:1] < live, key_row, GROUPS).astype(f32)
-    ones = jnp.ones((PAIRS, 128), bf16)
-    key_col = mm(jnp.where(pair_row == pair_col, key_row, 0.0).astype(bf16), ones)
-    wide = jnp.concatenate([key_col] * 4, axis=1)
-    ahead_of = (key_row < wide) | ((key_row == wide) & (pair_row < pair_col))
-    rank_col = mm(ahead_of.astype(f32).astype(bf16), ones)
-    group_row = lax.broadcasted_iota(jnp.int32, (PAIRS, 128), 1).astype(f32)
-    below_count = mm(jnp.ones((8, PAIRS), bf16), (key_col < group_row).astype(f32).astype(bf16))[:1]
-    gap = jnp.maximum(32.0 * (2.0 * group_row[:1] - 1.0), 0.0) - below_count
-    gap = jnp.where((group_row <= key_col) & (group_row < GROUPS), gap, 0.0)
-    place_col = rank_col + jnp.maximum(jnp.max(gap, axis=1, keepdims=True), 0.0)
-    place_col = jnp.where(key_col < GROUPS, place_col, 2.0 * PLACES)
-    number = lax.broadcasted_iota(jnp.int32, (8, PAIRS), 1)
-    row_of = lax.broadcasted_iota(jnp.int32, (8, PAIRS), 0)
-    digits = jnp.where(row_of == 0, number // 16, jnp.where(row_of == 1, lax.rem(number, 16), 1))
-    digits = digits.astype(f32).astype(bf16)
-    for n in range(PLACES // 128):
-        here = (place_col == group_row + n * 128.0).astype(f32).astype(bf16)
-        found = mm(digits, here)
-        order[:, pl.ds(n * 128, 128)] = jnp.where(
-            found[2:3] > 0.5, found[0:1] * 16.0 + found[1:2], -1.0
-        ).astype(jnp.int32)
-
-
-def place_call(slot, live):
-    vmem = pl.BlockSpec(memory_space=pltpu.VMEM)
-    return pl.pallas_call(
-        place_kernel,
-        out_shape=jax.ShapeDtypeStruct((1, PLACES), jnp.int32),
-        in_specs=[vmem, pl.BlockSpec(memory_space=pltpu.SMEM)],
-        out_specs=vmem,
-        name="places",
-    )(slot.reshape(1, PAIRS), live)
-
-
 def exchange_kernel(
-    count, depth, order_s, slot_s, rec_ref, ask_ref, tmp_ref, fwd_ref, inv_ref,
-    spec_out, rs_out, t_out, done_out,
-    rec32, asked, wanted, send, recv, halo_send, halo_recv, parts, part_energy, halo_spec,
-    spec, rs, temps, x0, x1, done,
+    count, depth, slot_s, rec_ref, ask_ref, tmp_ref, fwd_ref, inv_ref, slot_ref, live_s,
+    spec_out, rs_out, t_out, done_out, order_out,
+    rec32, asks, asked, wanted, send, recv, halo_send, halo_recv, parts, part_energy, halo_spec,
+    spec, rs, temps, order, order_s, x0, x1, done,
     ask_send_sem, ask_recv_sem, send_sem, recv_sem, halo_send_sem, halo_recv_sem, local_sem, done_sem, spec_sem, rs_sem,
 ):
     me = lax.axis_index("tmpl")
@@ -166,11 +122,19 @@
         return carry
 
     lax.fori_loop(0, 24, widen, 0)
+    rows = lax.broadcasted_iota(jnp.int32, (count, count), 0)
+    lanes = lax.broadcasted_iota(jnp.int32, (count, count), 1)
+    table = jnp.zeros((count, 128), jnp.int32)
+    for f in range(FETCH):
+        column = jnp.sum(jnp.where(rows == lanes, ask_ref[f:f + 1, :], 0), axis=1, keepdims=True)
+        table = jnp.where(lax.broadcasted_iota(jnp.int32, (count, 128), 1) == f, column, table)
+    for d in range(count):
+        asks[d] = table[d:d + 1, :]
     pl.semaphore_wait(barrier, count + 1)
 
     def ask_copy(i):
         return pltpu.make_async_remote_copy(
-            src_ref=ask_ref.at[ahead(i)], dst_ref=asked.at[i],
+            src_ref=asks.at[ahead(i)], dst_ref=asked.at[i],
             send_sem=ask_send_sem.at[i], recv_sem=ask_recv_sem.at[i],
             device_id={"tmpl": ahead(i)}, device_id_type=MESH,
         )
@@ -180,7 +144,7 @@
         return carry
 
     lax.fori_loop(1, count, ask_start, 0)
-    asked[0] = ask_ref[me]
+    asked[0] = asks[me]
 
     lane = lax.broadcasted_iota(jnp.int32, (128, 128), 1)
 
@@ -240,6 +204,35 @@
     out_t = pltpu.make_async_copy(temps, t_out, local_sem.at[1])
     out_t.start()
 
+    f32, bf16 = jnp.float32, jnp.bfloat16
+    i32 = jnp.int32
+    live = live_s[0]
+    pair_row = lax.broadcasted_iota(i32, (PAIRS, PAIRS), 1)
+    pair_col = lax.broadcasted_iota(i32, (PAIRS, PAIRS), 0)
+    source = lax.shift_right_logical(slot_ref[...], 2)
+    key_row = ((source + me) & 1) * 4 + ((lax.shift_right_logical(source, 3) - y) & 3)
+    key_row = jnp.where(pair_row[:1] < live, key_row, GROUPS)
+    key_col = jnp.sum(jnp.where(pair_row == pair_col, key_row, 0), axis=1, keepdims=True)
+    ahead_of = (key_row < key_col) | ((key_row == key_col) & (pair_row < pair_col))
+    rank_col = jnp.sum(ahead_of.astype(i32), axis=1, keepdims=True)
+    group_row = lax.broadcasted_iota(i32, (PAIRS, 128), 1)
+    below_count = jnp.sum((key_col < group_row).astype(i32), axis=0, keepdims=True)
+    gap = jnp.maximum(64 * group_row[:1] - 32, 0) - below_count
+    gap = jnp.where((group_row <= key_col) & (group_row < GROUPS), gap, 0)
+    place_col = rank_col + jnp.max(gap, axis=1, keepdims=True)
+    place_col = jnp.where(key_col < GROUPS, place_col, 2 * PLACES)
+    for n in range(PLACES // 128):
+        here = place_col == group_row + n * 128
+        found = jnp.sum(jnp.where(here, pair_col[:, :128] + 1, 0), axis=0, keepdims=True)
+        order[:, pl.ds(n * 128, 128)] = found - 1
+    order_copies = (
+        pltpu.make_async_copy(order, order_s, local_sem.at[0]),
+        pltpu.make_async_copy(order, order_out, local_sem.at[2]),
+    )
+    for copy in order_copies:
+        copy.start()
+    for copy in order_copies:
+        copy.wait()
     x1[...] = jnp.zeros_like(x1)
     lane8 = lax.broadcasted_iota(jnp.int32, (8, 128), 1)
 
@@ -411,7 +404,7 @@
     out_t.wait()
 
 
-def exchange_call(mesh, order, slot, rec, ask, templates, forward, inverse):
+def exchange_call(mesh, slot, rec, ask, templates, forward, inverse, live):
     count, depth = mesh.shape["tmpl"], mesh.shape["sta"]
     vmem = pl.BlockSpec(memory_space=pltpu.VMEM)
     hbm = pl.BlockSpec(memory_space=pl.ANY)
@@ -425,11 +418,13 @@
             jax.ShapeDtypeStruct((slots, 8, TL), f32),
             jax.ShapeDtypeStruct((512 * 32, 128), f32),
             jax.ShapeDtypeStruct((PAIRS + PB, 8, TL), f32),
+            jax.ShapeDtypeStruct((1, PLACES), jnp.int32),
         ],
-        in_specs=[smem] * 2 + [vmem] * 5,
-        out_specs=[hbm] * 4,
+        in_specs=[smem] + [vmem] * 6 + [smem],
+        out_specs=[hbm] * 5,
         scratch_shapes=[
             pltpu.VMEM((4, 768, 128), f32),
+            pltpu.VMEM((count, 1, 128), jnp.int32),
             pltpu.VMEM((count, 1, 128), jnp.int32),
             pltpu.SMEM((count, 1, 128), jnp.int32),
             pltpu.VMEM((count, ROWS, TL), bf16),
@@ -442,6 +437,8 @@
             pltpu.VMEM((slots * 3, 16, TL), bf16),
             pltpu.VMEM((slots, 8, TL), f32),
             pltpu.VMEM((512 * 32, 128), f32),
+            pltpu.VMEM((1, PLACES), jnp.int32),
+            pltpu.SMEM((1, PLACES), jnp.int32),
             pltpu.VMEM((PB * 8, NBINS), bf16),
             pltpu.VMEM((PB * 8, NBINS), bf16),
             pltpu.VMEM((PAIRS + PB, 8, TL), f32),
@@ -460,16 +457,17 @@
             collective_id=0, has_side_effects=True, vmem_limit_bytes=60 * 2**20
         ),
         name="exchange",
-    )(order, slot, rec, ask, templates, forward, inverse)
-
-
+    )(slot, rec, ask, templates, forward, inverse, slot.reshape(1, PAIRS), live)
+
+
+SUMS = 4
 CHUNKS = 8
 
 
 def pair_kernel(
     order_ref, slot_ref, tmpl_ref, off_ref, live_ref, inv_ref, pt_ref, spec_in, rs_in, t_in, done_in,
     out_ref, head_ref,
-    acc, done, x, y, spec, rs, temps, done_sem, spec_sem, rs_sem, t_sem,
+    sum0, sum1, sum2, sum3, done, x, y, spec, rs, temps, done_sem, spec_sem, rs_sem, t_sem,
 ):
     live = live_ref[0]
     lane = lax.broadcasted_iota(jnp.int32, (8, 128), 1)
@@ -482,9 +480,11 @@
 
     for n in range(CHUNKS):
         chunk(n).start()
-    acc[...] = jnp.zeros_like(acc)
-
-    def add(place, row):
+    sums = (sum0, sum1, sum2, sum3)
+    for acc in sums:
+        acc[...] = jnp.zeros_like(acc)
+
+    def add(place, row, acc):
         q = order_ref[0, place]
         j = jnp.where(q >= 0, tmpl_ref[jnp.maximum(q, 0)], T_DEV)
         o = off_ref[jnp.maximum(q, 0)]
@@ -501,7 +501,7 @@
 
     def add_some(b, carry):
         for i in range(8):
-            add(b * 8 + i, done[b * 8 + i])
+            add(b * 8 + i, done[b * 8 + i], sums[i % SUMS])
         return carry
 
     for n in range(CHUNKS):
@@ -532,7 +532,7 @@
             )
         y[...] = mm(x[...], inv_ref[...])
         for i in range(PB):
-            add(first + i, y[pl.ds(i * 8, 8), :] * rs[i])
+            add(first + i, y[pl.ds(i * 8, 8), :] * rs[i], sums[0])
 
     def late(n, carry):
         first = PAIRS + n * PB
@@ -552,13 +552,14 @@
     )
     counts = jnp.sum(same.astype(jnp.float32), axis=1, keepdims=True)
     scale = jnp.sqrt(SCALE / counts)
+    sum0[...] = (sum0[...] + sum1[...]) + (sum2[...] + sum3[...])
     for g in range(4):
         lanes = pl.ds(g * 128, 128)
-        head_ref[:, lanes] = acc[pl.ds(g * 8, T_DEV, stride=64), :] * scale
+        head_ref[:, lanes] = sum0[pl.ds(g * 8, T_DEV, stride=64), :] * scale
         for h in range(8):
-            v = acc[pl.ds(32 + g * 8 + h, T_DEV, stride=64), :]
+            v = sum0[pl.ds(32 + g * 8 + h, T_DEV, stride=64), :]
             if h < 7:
-                v = v + acc[pl.ds(g * 8 + h + 1, T_DEV, stride=64), :]
+                v = v + sum0[pl.ds(g * 8 + h + 1, T_DEV, stride=64), :]
             out_ref[h, :, lanes] = v * scale
 
 
@@ -573,7 +574,9 @@
         in_specs=[smem] * 5 + [vmem] * 2 + [hbm] * 4,
         out_specs=[vmem] * 2,
         scratch_shapes=[
-            pltpu.VMEM(((T_DEV + 1) * 64, 128), f32),
+        ]
+        + [pltpu.VMEM(((T_DEV + 1) * 64, 128), f32)] * SUMS
+        + [
             pltpu.VMEM((PAIRS, 8, TL), f32),
             pltpu.VMEM((PB * 8, NBINS), bf16),
             pltpu.VMEM((PB * 8, TL), f32),
@@ -585,7 +588,7 @@
             pltpu.SemaphoreType.DMA((PB,)),
             pltpu.SemaphoreType.DMA((PB,)),
         ],
-        compiler_params=pltpu.CompilerParams(vmem_limit_bytes=40 * 2**20),
+        compiler_params=pltpu.CompilerParams(vmem_limit_bytes=60 * 2**20),
         name="pairs",
     )(order, slot, tmpl, off, live, inverse, tmpl.reshape(1, PAIRS), spec, rs, t, done)
 
@@ -593,11 +596,10 @@
 def shards(mesh, records, templates, requests, pair_slot, pair_template, pair_offset, live_pairs):
     count, depth = mesh.shape["tmpl"], mesh.shape["sta"]
     rec = jnp.transpose(records, (0, 2, 1, 3)).reshape(24, 32, TL)
-    ask = jnp.pad(requests.reshape(count, 1, FETCH), ((0, 0), (0, 0), (0, 128 - FETCH)))
-    order = place_call(pair_slot, live_pairs)
-    spec, rs, temps, done = exchange_call(
-        mesh, order, pair_slot, rec, ask, jnp.transpose(templates, (1, 0, 2)), jnp.asarray(FORWARD),
-        jnp.asarray(INVERSE),
+    ask = jnp.transpose(requests.reshape(count, FETCH))
+    spec, rs, temps, done, order = exchange_call(
+        mesh, pair_slot, rec, ask, jnp.transpose(templates, (1, 0, 2)), jnp.asarray(FORWARD),
+        jnp.asarray(INVERSE), live_pairs,
     )
     out, head = pair_call(
         order, pair_slot, pair_template, pair_offset, live_pairs, jnp.asarray(INVERSE), spec, rs, temps, done

time: 106 us -> 93.7 us (0.88)
  local copies, waits for them, and re-layouts: 9.7 us -> 0 us
  Pallas kernels: 88.6 us -> 86.2 us
    unnamed x14 -> x0, local copies, waits for them, and re-layouts: 8.32 us -> none
    pallas_call x1 -> x0, Pallas kernels: 2.37 us -> none  [place_call(): pl.pallas_call(place_kernel, out_shape=jax.ShapeDtypeStruct((1, PLACES),...]
where the time goes in v3:
time: 93.7 us; the launch traced here: 93.5 us
  Pallas kernels  86.2 us (92%)
  waiting for transfers between devices  3.92 us (4%)
  other arithmetic  1.48 us (2%)
  starting transfers between devices  1.29 us (1%)
    pallas_call x1, Pallas kernels, exchange_call(): pl.pallas_call(functools.partial(exchange_kernel, count, depth), out_shap...  74.4 us
    pallas_call x1, Pallas kernels, pair_call(): pl.pallas_call(pair_kernel, out_shape=[jax.ShapeDtypeStruct((8, T_DEV, TL...  11.8 us
    ppermute x1, waiting for transfers between devices, shards(): head = lax.ppermute(head, 'sta', [(i, i - 1) for i in range(1, depth)])  3.92 us
  transfers between devices with their start and end apart: 1, of which 1 were waited for; matrix products, arithmetic and copies ran while one was open for 0% of the time, Pallas kernels for 0%

profile of v3, /device:TPU:7, one launch (start us, length us, event | category | flops | bytes accessed | tf_op | source)
XLA Modules:
  0.0 93.5 jit_solution(12034822251376534584)
XLA Ops:
  0.7 74.4 %exchange.1 = (bf16[384,16,512]{2,1,0:T(8,128)(2,1)}, f32[128,8,512]{2,1,0:T(8,128)}, f32[16384,128]{1,0:T(8,128)}, f32[528,8,512]{2,1,0:T(8,128)}, s32[1,1024]{1,0:T(1,128)}) custom-call(s32[512]{0:T(512)} %slot_ref.1, bf16[24,32,512]{2,1,0:T(8,128)(2,1)} %bitcast.14, s32[4,32]{1,0:T(4,128)} %bitcast.17, bf16[3,512,512]{2,1,0:T(8,128)(2,1)} %bitcast.13, ...), custom_call_target="tpu_custom_call" | custom-call | tf_op jit(solution)/shard_map/exchange/pallas_call | solution.py:414
  75.1 11.8 %pairs.1 = (f32[8,32,512]{2,1,0:T(8,128)}, f32[32,512]{1,0:T(8,128)}) custom-call(s32[1,1024]{1,0:T(1,128)} %get-tuple-element.24.order_ref, s32[512]{0:T(512)} %slot_ref.1, s32[512]{0:T(512)} %tmpl_ref.1, s32[512]{0:T(512)} %off_ref.1, s32[1]{0:T(128)S(6)} %copy.11.live_s.live_ref, bf16[1024,512]{1,0:T(8,128)(2,1)} %constant.34.clone.inv_ref, ...), custom_call_target="tpu_custom_call" | custom-call | tf_op jit(solution)/shard_map/pairs/pallas_call | solution.py:571
  86.8 1.3 %collective-permute-start = (f32[32,512]{1,0:T(8,128)}, f32[32,512]{1,0:T(8,128)S(1)}, u32[]{:S(2)}, u32[]{:S(2)}) collective-permute-start(f32[32,512]{1,0:T(8,128)} %get-tuple-element.30), channel_id=1, source_target_pairs={{1,0},{2,1},{3,2},{4,3},{5,4},{6,5},{7,6},{9,8},{10,9},{11,10},{12... | collective-permute-start | bytes 196616 | tf_op jit(solution)/shard_map/ppermute | solution.py:607
  88.1 3.9 %collective-permute-done = f32[32,512]{1,0:T(8,128)S(1)} collective-permute-done((f32[32,512]{1,0:T(8,128)}, f32[32,512]{1,0:T(8,128)S(1)}, u32[]{:S(2)}, u32[]{:S(2)}) %collective-permute-start) | collective-permute-done | bytes 65568 | tf_op jit(solution)/shard_map/ppermute | solution.py:607
  92.1 1.5 %fusion = f32[8,32,512]{2,1,0:T(8,128)} fusion(f32[8,32,512]{2,1,0:T(8,128)} %get-tuple-element.29, f32[32,512]{1,0:T(8,128)S(1)} %collective-permute-done), kind=kLoop, calls=%fused_computation.1 | loop fusion | flops 16384 | bytes 196608 | tf_op jit(solution)/shard_map/scatter-add | solution.py:608
Async XLA Ops:
  86.8 5.2 %collective-permute-start = (f32[32,512]{1,0:T(8,128)}, f32[32,512]{1,0:T(8,128)S(1)}, u32[]{:S(2)}, u32[]{:S(2)}) collective-permute-start(f32[32,512]{1,0:T(8,128)} %get-tuple-element.30), channel_id=1, source_target_pairs={{1,0},{2,1},{3,2},{4,3},{5,4},{6,5},{7,6},{9,8},{10,9},{11,10},{12... | collective-permute-start | bytes 196616 | tf_op jit(solution)/shard_map/ppermute | solution.py:607

commit v4 on v3

--- a/solution.py
+++ b/solution.py
@@ -78,10 +78,10 @@
 
 
 def exchange_kernel(
-    count, depth, slot_s, rec_ref, ask_ref, tmp_ref, fwd_ref, inv_ref, slot_ref, live_s,
-    spec_out, rs_out, t_out, done_out, order_out,
+    count, depth, slot_s, rec_ref, ask_ref, tmp_ref, fwd_ref, inv_ref, slot_ref, tmpl_ref, off_ref, live_s,
+    spec_out, rs_out, t_out, done_out, order_out, codes_out,
     rec32, asks, asked, wanted, send, recv, halo_send, halo_recv, parts, part_energy, halo_spec,
-    spec, rs, temps, order, order_s, x0, x1, done,
+    spec, rs, temps, order, codes, order_s, x0, x1, done,
     ask_send_sem, ask_recv_sem, send_sem, recv_sem, halo_send_sem, halo_recv_sem, local_sem, done_sem, spec_sem, rs_sem,
 ):
     me = lax.axis_index("tmpl")
@@ -159,50 +159,11 @@
                 base = n * 4096 + g * 8
                 temps[pl.ds(base + c, 128, stride=32), :] = found[:, g * 128:(g + 1) * 128]
                 temps[pl.ds(base + c + 3, 128, stride=32), :] = found[:, TL + g * 128:TL + (g + 1) * 128]
-        for g in range(4):
-            for row in (6, 7):
-                temps[pl.ds(n * 4096 + g * 8 + row, 128, stride=32), :] = jnp.zeros((128, 128), jnp.float32)
         return carry
 
     def ask_wait(i, carry):
         ask_copy(i).wait()
         return carry
-
-    lax.fori_loop(1, count, ask_wait, 0)
-    to_scalar = pltpu.make_async_copy(asked, wanted, local_sem.at[0])
-    to_scalar.start()
-    to_scalar.wait()
-
-    def gather(i):
-        rows = []
-        for f in range(FETCH):
-            s = wanted[i, 0, f]
-            for c in range(3):
-                rows.append(
-                    jnp.concatenate(
-                        [rec32[g, pl.ds(c * 32 + s, 8, stride=96), :] for g in range(4)], axis=1
-                    )
-                )
-        return jnp.concatenate(rows, axis=0).astype(jnp.bfloat16)
-
-    def data_copy(i):
-        return pltpu.make_async_remote_copy(
-            src_ref=send.at[i], dst_ref=recv.at[i],
-            send_sem=send_sem.at[i], recv_sem=recv_sem.at[i],
-            device_id={"tmpl": behind(i)}, device_id_type=MESH,
-        )
-
-    def data_start(i, carry):
-        send[i] = gather(i)
-        data_copy(i).start()
-        return carry
-
-    lax.fori_loop(1, count, data_start, 0)
-    recv[0] = gather(0)
-
-    lax.fori_loop(0, 4, template_block, 0)
-    out_t = pltpu.make_async_copy(temps, t_out, local_sem.at[1])
-    out_t.start()
 
     f32, bf16 = jnp.float32, jnp.bfloat16
     i32 = jnp.int32
@@ -219,20 +180,62 @@
     below_count = jnp.sum((key_col < group_row).astype(i32), axis=0, keepdims=True)
     gap = jnp.maximum(64 * group_row[:1] - 32, 0) - below_count
     gap = jnp.where((group_row <= key_col) & (group_row < GROUPS), gap, 0)
+    code_row = (tmpl_ref[...] * 64 + 24 - 8 * lax.shift_right_logical(off_ref[...], 7)) * 128 + (off_ref[...] & 127)
+    code_col = jnp.sum(jnp.where(pair_row == pair_col, code_row, 0), axis=1, keepdims=True)
     place_col = rank_col + jnp.max(gap, axis=1, keepdims=True)
     place_col = jnp.where(key_col < GROUPS, place_col, 2 * PLACES)
     for n in range(PLACES // 128):
         here = place_col == group_row + n * 128
         found = jnp.sum(jnp.where(here, pair_col[:, :128] + 1, 0), axis=0, keepdims=True)
         order[:, pl.ds(n * 128, 128)] = found - 1
+        code = jnp.sum(jnp.where(here, code_col, 0), axis=0, keepdims=True)
+        codes[:, pl.ds(n * 128, 128)] = jnp.where(found > 0, code, (T_DEV * 64 + 24) * 128)
     order_copies = (
-        pltpu.make_async_copy(order, order_s, local_sem.at[0]),
+        pltpu.make_async_copy(order, order_s, local_sem.at[4]),
         pltpu.make_async_copy(order, order_out, local_sem.at[2]),
+        pltpu.make_async_copy(codes, codes_out, local_sem.at[5]),
     )
     for copy in order_copies:
         copy.start()
+    lax.fori_loop(0, 2, template_block, 0)
+    lax.fori_loop(1, count, ask_wait, 0)
+    to_scalar = pltpu.make_async_copy(asked, wanted, local_sem.at[0])
+    to_scalar.start()
+    to_scalar.wait()
+
+    def gather(i):
+        rows = []
+        for f in range(FETCH):
+            s = wanted[i, 0, f]
+            for c in range(3):
+                rows.append(
+                    jnp.concatenate(
+                        [rec32[g, pl.ds(c * 32 + s, 8, stride=96), :] for g in range(4)], axis=1
+                    )
+                )
+        return jnp.concatenate(rows, axis=0).astype(jnp.bfloat16)
+
+    def data_copy(i):
+        return pltpu.make_async_remote_copy(
+            src_ref=send.at[i], dst_ref=recv.at[i],
+            send_sem=send_sem.at[i], recv_sem=recv_sem.at[i],
+            device_id={"tmpl": behind(i)}, device_id_type=MESH,
+        )
+
+    def data_start(i, carry):
+        send[i] = gather(i)
+        data_copy(i).start()
+        return carry
+
+    lax.fori_loop(1, count, data_start, 0)
+    recv[0] = gather(0)
+
     for copy in order_copies:
         copy.wait()
+    lax.fori_loop(2, 4, template_block, 0)
+    out_t = pltpu.make_async_copy(temps, t_out, local_sem.at[1])
+    out_t.start()
+
     x1[...] = jnp.zeros_like(x1)
     lane8 = lax.broadcasted_iota(jnp.int32, (8, 128), 1)
 
@@ -346,7 +349,7 @@
                 rs[station_at(g, s), :, columns] = lax.rsqrt(total / SCALE + EPSILON)
             return carry
 
-        lax.fori_loop(0, 16, station, 0)
+        lax.fori_loop(0, 16, station, 0, unroll=2)
 
         def leave(k, carry):
             spec_copy(g * PER + k).start()
@@ -404,7 +407,7 @@
     out_t.wait()
 
 
-def exchange_call(mesh, slot, rec, ask, templates, forward, inverse, live):
+def exchange_call(mesh, slot, rec, ask, templates, forward, inverse, tmpl, off, live):
     count, depth = mesh.shape["tmpl"], mesh.shape["sta"]
     vmem = pl.BlockSpec(memory_space=pltpu.VMEM)
     hbm = pl.BlockSpec(memory_space=pl.ANY)
@@ -419,9 +422,10 @@
             jax.ShapeDtypeStruct((512 * 32, 128), f32),
             jax.ShapeDtypeStruct((PAIRS + PB, 8, TL), f32),
             jax.ShapeDtypeStruct((1, PLACES), jnp.int32),
+            jax.ShapeDtypeStruct((1, PLACES), jnp.int32),
         ],
-        in_specs=[smem] + [vmem] * 6 + [smem],
-        out_specs=[hbm] * 5,
+        in_specs=[smem] + [vmem] * 8 + [smem],
+        out_specs=[hbm] * 6,
         scratch_shapes=[
             pltpu.VMEM((4, 768, 128), f32),
             pltpu.VMEM((count, 1, 128), jnp.int32),
@@ -438,6 +442,7 @@
             pltpu.VMEM((slots, 8, TL), f32),
             pltpu.VMEM((512 * 32, 128), f32),
             pltpu.VMEM((1, PLACES), jnp.int32),
+            pltpu.VMEM((1, PLACES), jnp.int32),
             pltpu.SMEM((1, PLACES), jnp.int32),
             pltpu.VMEM((PB * 8, NBINS), bf16),
             pltpu.VMEM((PB * 8, NBINS), bf16),
@@ -448,7 +453,7 @@
             pltpu.SemaphoreType.DMA((count,)),
             pltpu.SemaphoreType.DMA((GROUPS,)),
             pltpu.SemaphoreType.DMA((GROUPS,)),
-            pltpu.SemaphoreType.DMA((4,)),
+            pltpu.SemaphoreType.DMA((6,)),
             pltpu.SemaphoreType.DMA((PAIRS // 32,)),
             pltpu.SemaphoreType.DMA((count,)),
             pltpu.SemaphoreType.DMA((count,)),
@@ -457,7 +462,10 @@
             collective_id=0, has_side_effects=True, vmem_limit_bytes=60 * 2**20
         ),
         name="exchange",
-    )(slot, rec, ask, templates, forward, inverse, slot.reshape(1, PAIRS), live)
+    )(
+        slot, rec, ask, templates, forward, inverse, slot.reshape(1, PAIRS), tmpl.reshape(1, PAIRS),
+        off.reshape(1, PAIRS), live,
+    )
 
 
 SUMS = 4
@@ -465,9 +473,9 @@
 
 
 def pair_kernel(
-    order_ref, slot_ref, tmpl_ref, off_ref, live_ref, inv_ref, pt_ref, spec_in, rs_in, t_in, done_in,
+    order_ref, codes_ref, slot_ref, live_ref, pt_ref, inv_in, spec_in, rs_in, t_in, done_in,
     out_ref, head_ref,
-    sum0, sum1, sum2, sum3, done, x, y, spec, rs, temps, done_sem, spec_sem, rs_sem, t_sem,
+    sum0, sum1, sum2, sum3, done, x, y, spec, rs, temps, inv_ref, inv_sem, done_sem, spec_sem, rs_sem, t_sem,
 ):
     live = live_ref[0]
     lane = lax.broadcasted_iota(jnp.int32, (8, 128), 1)
@@ -485,28 +493,25 @@
         acc[...] = jnp.zeros_like(acc)
 
     def add(place, row, acc):
-        q = order_ref[0, place]
-        j = jnp.where(q >= 0, tmpl_ref[jnp.maximum(q, 0)], T_DEV)
-        o = off_ref[jnp.maximum(q, 0)]
-        coarse = lax.shift_right_logical(o, 7)
-        fine = o & 127
+        code = codes_ref[0, place]
+        fine = code & 127
         low = lane < 128 - fine
         turned = [pltpu.roll(row[:, g * 128:(g + 1) * 128], 128 - fine, 1) for g in range(4)]
         parts = [jnp.where(low, 0.0, turned[0])]
         for g in range(3):
             parts.append(jnp.where(low, turned[g], turned[g + 1]))
         parts.append(jnp.where(low, turned[3], 0.0))
-        base = pl.multiple_of(j * 64 + 24 - 8 * coarse, 8)
+        base = pl.multiple_of(lax.shift_right_logical(code, 7), 8)
         acc[pl.ds(base, 40), :] += jnp.concatenate(parts, axis=0)
 
     def add_some(b, carry):
-        for i in range(8):
-            add(b * 8 + i, done[b * 8 + i], sums[i % SUMS])
+        for i in range(16):
+            add(b * 16 + i, done[b * 16 + i], sums[i % SUMS])
         return carry
 
     for n in range(CHUNKS):
         chunk(n).wait()
-        lax.fori_loop(n * (PAIRS // CHUNKS // 8), (n + 1) * (PAIRS // CHUNKS // 8), add_some, 0)
+        lax.fori_loop(n * (PAIRS // CHUNKS // 16), (n + 1) * (PAIRS // CHUNKS // 16), add_some, 0)
 
     def copies(q, i):
         s = slot_ref[q]
@@ -545,6 +550,9 @@
 
     @pl.when(order_ref[0, PAIRS] >= 0)
     def _():
+        table = pltpu.make_async_copy(inv_in, inv_ref, inv_sem)
+        table.start()
+        table.wait()
         lax.fori_loop(0, (PLACES - PAIRS) // PB, late, 0)
 
     same = (pt_ref[...] == lax.broadcasted_iota(jnp.int32, (T_DEV, PAIRS), 0)) & (
@@ -563,7 +571,7 @@
             out_ref[h, :, lanes] = v * scale
 
 
-def pair_call(order, slot, tmpl, off, live, inverse, spec, rs, t, done):
+def pair_call(order, codes, slot, tmpl, live, inverse, spec, rs, t, done):
     smem = pl.BlockSpec(memory_space=pltpu.SMEM)
     vmem = pl.BlockSpec(memory_space=pltpu.VMEM)
     hbm = pl.BlockSpec(memory_space=pl.ANY)
@@ -571,7 +579,7 @@
     return pl.pallas_call(
         pair_kernel,
         out_shape=[jax.ShapeDtypeStruct((8, T_DEV, TL), f32), jax.ShapeDtypeStruct((T_DEV, TL), f32)],
-        in_specs=[smem] * 5 + [vmem] * 2 + [hbm] * 4,
+        in_specs=[smem] * 4 + [vmem] + [hbm] * 5,
         out_specs=[vmem] * 2,
         scratch_shapes=[
         ]
@@ -583,6 +591,8 @@
             pltpu.VMEM((PB, 3, 16, TL), bf16),
             pltpu.VMEM((PB, 8, TL), f32),
             pltpu.VMEM((PB, 32, 128), f32),
+            pltpu.VMEM((NBINS, TL), bf16),
+            pltpu.SemaphoreType.DMA,
             pltpu.SemaphoreType.DMA((CHUNKS,)),
             pltpu.SemaphoreType.DMA((PB,)),
             pltpu.SemaphoreType.DMA((PB,)),
@@ -590,19 +600,19 @@
         ],
         compiler_params=pltpu.CompilerParams(vmem_limit_bytes=60 * 2**20),
         name="pairs",
-    )(order, slot, tmpl, off, live, inverse, tmpl.reshape(1, PAIRS), spec, rs, t, done)
+    )(order, codes, slot, live, tmpl.reshape(1, PAIRS), inverse, spec, rs, t, done)
 
 
 def shards(mesh, records, templates, requests, pair_slot, pair_template, pair_offset, live_pairs):
     count, depth = mesh.shape["tmpl"], mesh.shape["sta"]
     rec = jnp.transpose(records, (0, 2, 1, 3)).reshape(24, 32, TL)
     ask = jnp.transpose(requests.reshape(count, FETCH))
-    spec, rs, temps, done, order = exchange_call(
+    spec, rs, temps, done, order, codes = exchange_call(
         mesh, pair_slot, rec, ask, jnp.transpose(templates, (1, 0, 2)), jnp.asarray(FORWARD),
-        jnp.asarray(INVERSE), live_pairs,
+        jnp.asarray(INVERSE), pair_template, pair_offset, live_pairs,
     )
     out, head = pair_call(
-        order, pair_slot, pair_template, pair_offset, live_pairs, jnp.asarray(INVERSE), spec, rs, temps, done
+        order, codes, pair_slot, pair_template, live_pairs, jnp.asarray(INVERSE), spec, rs, temps, done
     )
     head = lax.ppermute(head, "sta", [(i, i - 1) for i in range(1, depth)])
     return out.at[7].add(head)

time: 93.7 us -> 91.5 us (0.977)
  Pallas kernels: 86.2 us -> 83.1 us
    pallas_call x1, Pallas kernels: 11.8 us -> 9.05 us  [pair_call(): pl.pallas_call(pair_kernel, out_shape=[jax.ShapeDtypeStruct((8, T_DEV, TL...]
where the time goes in v4:
time: 91.5 us; the launch traced here: 90.4 us
  Pallas kernels  83.1 us (91%)
  waiting for transfers between devices  3.92 us (4%)
  other arithmetic  1.48 us (2%)
  starting transfers between devices  1.29 us (1%)
    pallas_call x1, Pallas kernels, exchange_call(): pl.pallas_call(functools.partial(exchange_kernel, count, depth), out_shap...  74 us
    pallas_call x1, Pallas kernels, pair_call(): pl.pallas_call(pair_kernel, out_shape=[jax.ShapeDtypeStruct((8, T_DEV, TL...  9.05 us
    ppermute x1, waiting for transfers between devices, shards(): head = lax.ppermute(head, 'sta', [(i, i - 1) for i in range(1, depth)])  3.92 us
  transfers between devices with their start and end apart: 1, of which 1 were waited for; matrix products, arithmetic and copies ran while one was open for 0% of the time, Pallas kernels for 0%

profile of v4, /device:TPU:7, one launch (start us, length us, event | category | flops | bytes accessed | tf_op | source)
XLA Modules:
  0.0 90.4 jit_solution(18134921154325090179)
XLA Ops:
  0.7 74.0 %exchange.1 = (bf16[384,16,512]{2,1,0:T(8,128)(2,1)}, f32[128,8,512]{2,1,0:T(8,128)}, f32[16384,128]{1,0:T(8,128)}, f32[528,8,512]{2,1,0:T(8,128)}, s32[1,1024]{1,0:T(1,128)}, /*index=5*/s32[1,1024]{1,0:T(1,128)}) custom-call(s32[512]{0:T(512)} %slot_ref.1, bf16[24,32,512]{2,1,0:T(8,128)(2,1)} %bitcast.15, s32[4,32]{1,0:T(4,128)} %bitcast.19, ...), custom_call_target="tpu_custom_call" | custom-call | tf_op jit(solution)/shard_map/exchange/pallas_call | solution.py:417
  74.7 9.0 %pairs.1 = (f32[8,32,512]{2,1,0:T(8,128)}, f32[32,512]{1,0:T(8,128)}) custom-call(s32[1,1024]{1,0:T(1,128)} %get-tuple-element.25.order_ref, s32[1,1024]{1,0:T(1,128)} %get-tuple-element.26.codes_ref, s32[512]{0:T(512)} %slot_ref.1, s32[1]{0:T(128)S(6)} %copy.11.live_s.live_ref, s32[1,512]{1,0:T(1,128)} %bitcast.18, ...), custom_call_target="tpu_custom_call" | custom-call | tf_op jit(solution)/shard_map/pairs/pallas_call | solution.py:579
  83.7 1.3 %collective-permute-start = (f32[32,512]{1,0:T(8,128)}, f32[32,512]{1,0:T(8,128)S(1)}, u32[]{:S(2)}, u32[]{:S(2)}) collective-permute-start(f32[32,512]{1,0:T(8,128)} %get-tuple-element.32), channel_id=1, source_target_pairs={{1,0},{2,1},{3,2},{4,3},{5,4},{6,5},{7,6},{9,8},{10,9},{11,10},{12... | collective-permute-start | bytes 196616 | tf_op jit(solution)/shard_map/ppermute | solution.py:617
  85.0 3.9 %collective-permute-done = f32[32,512]{1,0:T(8,128)S(1)} collective-permute-done((f32[32,512]{1,0:T(8,128)}, f32[32,512]{1,0:T(8,128)S(1)}, u32[]{:S(2)}, u32[]{:S(2)}) %collective-permute-start) | collective-permute-done | bytes 65568 | tf_op jit(solution)/shard_map/ppermute | solution.py:617
  88.9 1.5 %fusion = f32[8,32,512]{2,1,0:T(8,128)} fusion(f32[8,32,512]{2,1,0:T(8,128)} %get-tuple-element.31, f32[32,512]{1,0:T(8,128)S(1)} %collective-permute-done), kind=kLoop, calls=%fused_computation.1 | loop fusion | flops 16384 | bytes 196608 | tf_op jit(solution)/shard_map/scatter-add | solution.py:618
Async XLA Ops:
  83.7 5.2 %collective-permute-start = (f32[32,512]{1,0:T(8,128)}, f32[32,512]{1,0:T(8,128)S(1)}, u32[]{:S(2)}, u32[]{:S(2)}) collective-permute-start(f32[32,512]{1,0:T(8,128)} %get-tuple-element.32), channel_id=1, source_target_pairs={{1,0},{2,1},{3,2},{4,3},{5,4},{6,5},{7,6},{9,8},{10,9},{11,10},{12... | collective-permute-start | bytes 196616 | tf_op jit(solution)/shard_map/ppermute | solution.py:617
